TPU v7x, 128 devices: a whole 4x4x4 slice. The times are simulated.
128 devices in a mesh: dp: 16 (over x, z), row: 4 (over y_hi, core), col: 2 (over y_lo).
Axes of the slice: x: 4, y: 4 (y_hi: 2, y_lo: 2; y = y_hi * 2 + y_lo), z: 4, core: 2. Of those that a mesh axis runs over, the one named last changes fastest.
Arguments:
- atom_feats: bfloat16 [2, 1024, 32, 1024], P(None, 'dp'), may hold values from -6 to 6
- atom_bead: int32 [2, 1024, 32], P(None, 'dp'), may hold values from 0 to 15, as said below
- bead_count: int32 [2, 1024], P(None, 'dp'), may hold values from 8 to 16
- bead_type: int32 [2, 1024, 16], P(None, 'dp'), may hold values from 0 to 3
- sparse_points: bfloat16 [8192, 1024], P(('row', 'col')), may hold values from -6 to 6
- sparse_type: int32 [8192], P(('row', 'col')), may hold values from 0 to 3
- targets: float32 [2, 3, 1024], P(None, None, 'dp'), may hold values from -6 to 6
Outputs:
- gram: float32 [8192, 4, 2048], P(('row', 'dp'), None, 'col')
- rhs: float32 [3, 8192], P(None, ('row', 'col'))
Inputs may be any that keep to these rules, and one draw needn't show every extreme that they name: `atom_bead`: in every configuration the atoms map to beads below its bead count, and every bead below the count holds at least one atom.
All inputs are finite; a program needn't handle non-finite values.
Results may differ from a plain program's by a relative error of at most 0.012.
Values may be sent and summed in bfloat16 or wider, within the bound.
A program may use at most 128 MiB of HBM per device.

v0:
```python
import jax
import jax.numpy as jnp
from jax import lax
from jax.sharding import PartitionSpec as P

EPSILON = 1e-06


def unit_rows(values):
    widened = values.astype(jnp.float32)
    scale = jnp.sqrt(jnp.mean(widened * widened, axis=-1, keepdims=True) + EPSILON)
    return (widened / scale).astype(jnp.bfloat16)


def bead_units(atom_feats, atom_bead, beads):
    slots = jnp.arange(beads, dtype=jnp.int32)
    onehot = (atom_bead[:, :, None, :] == slots[None, None, :, None]).astype(jnp.bfloat16)
    summed = jnp.einsum("sgba,sgad->sgbd", onehot, atom_feats, preferred_element_type=jnp.float32)
    bead_sizes = jnp.sum(onehot.astype(jnp.float32), axis=-1)
    return unit_rows(summed / jnp.maximum(bead_sizes, 1.0)[..., None])


def kernel_block(bead_unit, live_type, points, point_type):
    config_rows, beads, width = bead_unit.shape
    scores = jnp.einsum(
        "rd,md->rm",
        bead_unit.reshape(config_rows * beads, width),
        points,
        preferred_element_type=jnp.float32,
    )
    scores = (scores * width ** (-0.5)).reshape(config_rows, beads, points.shape[0])
    match = live_type[:, :, None] == point_type[None, None, :]
    values = jnp.where(match, jnp.exp(scores), jnp.zeros_like(scores))
    return jnp.sum(values, axis=1)


def shards(atom_feats, atom_bead, bead_count, bead_type, sparse_points, sparse_type, targets):
    slabs, local, atoms, width = atom_feats.shape
    beads = bead_type.shape[-1]
    config_rows = slabs * local
    units = bead_units(atom_feats, atom_bead, beads).reshape(config_rows, beads, width)
    slots = jnp.arange(beads, dtype=jnp.int32)
    live_type = jnp.where(slots[None, None, :] < bead_count[:, :, None], bead_type, -1).reshape(
        config_rows, beads
    )
    point_unit = unit_rows(sparse_points)
    shard = sparse_points.shape[0]
    total = config_rows * lax.axis_size("dp")

    def place_kernel(parts):
        block = kernel_block(units, live_type, parts[0], parts[1])
        return block

    row_kernel = place_kernel(
        (
            lax.all_gather(point_unit, "col", axis=0, tiled=True),
            lax.all_gather(sparse_type, "col", axis=0, tiled=True),
        )
    ).astype(jnp.bfloat16)
    col_kernel = place_kernel(
        (
            lax.all_gather(point_unit, "row", axis=0, tiled=True),
            lax.all_gather(sparse_type, "row", axis=0, tiled=True),
        )
    ).astype(jnp.bfloat16)
    own_kernel = lax.dynamic_slice_in_dim(row_kernel, lax.axis_index("col") * shard, shard, 1)
    weights = jnp.transpose(targets, (1, 0, 2)).reshape(3, config_rows)
    partial_rhs = jnp.dot(weights, own_kernel.astype(jnp.float32), precision=lax.Precision.HIGHEST)
    rhs = lax.psum(partial_rhs, "dp") / total
    own_rows = row_kernel.shape[1] // lax.axis_size("dp")
    contract = (((0,), (0,)), ((), ()))
    gram_local = lax.psum_scatter(
        lax.dot_general(
            row_kernel, col_kernel, contract, preferred_element_type=jnp.float32
        ).astype(jnp.bfloat16),
        "dp",
        scatter_dimension=0,
        tiled=True,
    ).astype(jnp.float32)
    gram = (gram_local / total).reshape(own_rows, lax.axis_size("row"), shard)
    return (gram, rhs)


def solution(mesh):
    return jax.shard_map(
        shards,
        mesh=mesh,
        in_specs=(
            P(None, "dp", None, None),
            P(None, "dp", None),
            P(None, "dp"),
            P(None, "dp", None),
            P(("row", "col"), None),
            P(("row", "col")),
            P(None, None, "dp"),
        ),
        out_specs=(P(("row", "dp"), None, "col"), P(None, ("row", "col"))),
        check_vma=False,
    )
```

profile of v0, /device:TPU:1, one launch (start us, length us, event | category | flops | bytes accessed | tf_op | source)
XLA Modules:
  0.0 299.4 jit_solution(7742784095340806613)
XLA Ops:
  7.2 0.0 copy-start
  7.2 0.0 copy-start.2
  7.2 0.0 copy-start.4
  7.2 0.0 copy-start.1
  7.2 0.0 all-gather.3.cloned.1.call-start
  7.3 2.1 fusion
  9.3 3.7 %fusion.1 = bf16[1024,1024]{1,0:T(8,128)(2,1)} fusion(bf16[1024,1024]{1,0:T(8,128)(2,1)} %param.11, f32[1024]{0:T(1024)S(1)} %add_sqrt_fusion), kind=kLoop, calls=%fused_computation.10 | loop fusion | flops 3145728 | bytes 4198400 | tf_op jit(solution)/shard_map/convert_element_type | solution.py:12
  13.1 0.0 all-gather.3.cloned.1.call-update
  13.1 0.0 all-gather.5.cloned.1.call-start
  13.1 0.7 all-gather.5.cloned.1.call-update
  13.8 0.0 reduce-scatter.2.cloned.1.call-start
  13.9 0.0 copy-done
  13.9 0.1 copy.16
  14.0 0.0 copy-done.2
  14.0 0.0 copy-done.4
  14.0 0.1 copy.18
  14.1 0.0 copy-done.1
  14.1 3.8 %all_gather.12 = s32[2048]{0:T(1024)S(1)} all-gather(s32[1024]{0:T(1024)S(1)} %copy-done.1), channel_id=1, replica_groups=mesh['dp'=16,'row'=4,'col'=2] {'col'}, dimensions={0}, use_global_device_ids=true | all-gather | bytes 12288 | tf_op jit(solution)/shard_map/all_gather | solution.py:57
  17.9 8.4 %all_gather.14 = s32[4096]{0:T(1024)S(1)} all-gather(s32[1024]{0:T(1024)S(1)} %copy-done.1), channel_id=1, replica_groups=mesh['dp'=16,'row'=4,'col'=2] {'row'}, dimensions={0}, use_global_device_ids=true | all-gather | bytes 20480 | tf_op jit(solution)/shard_map/all_gather | solution.py:63
  26.3 0.3 convert_reduce_fusion
  26.7 5.6 %multiply_reduce_fusion = (f32[2,64,16]{2,1,0:T(8,128)S(1)}, f32[2,64,16,1024]{3,2,1,0:T(8,128)S(1)}) fusion(f32[2,64,16]{2,1,0:T(8,128)S(1)} %broadcast_maximum_fusion, bf16[2,64,32,1024]{3,2,1,0:T(8,128)(2,1)} %param.7, s32[2,64,32]{2,1,0:T(8,128)S(1)} %copy.16), kind=kOutput, calls=%fused_computation.6 | convolution fusion | flops 140572672 | bytes 16809984 | tf_op jit(solution)/shard_map/sgba,sgad->sgbd/dot_general | solution.py:18
  32.3 2.5 divide_convert_fusion
  34.9 40.9 %all-gather.3.cloned.1.call-done = bf16[2048,1024]{1,0:T(8,128)(2,1)} async-done(((bf16[1024,1024]{1,0:T(8,128)(2,1)}), bf16[2048,1024]{1,0:T(8,128)(2,1)}) %all-gather.3.cloned.1.call-update) | async-done | bytes 4194320 | tf_op jit(solution)/shard_map/all_gather | solution.py:56
  75.8 14.6 %select_reduce_fusion.1 = bf16[128,2048]{1,0:T(8,128)(2,1)S(1)} fusion(s32[2048]{0:T(1024)S(1)} %all_gather.12, s32[128,16]{1,0:T(8,128)S(1)} %bitcast.19, bf16[2048,1024]{1,0:T(8,128)(2,1)} %bitcast.17, bf16[2048,1024]{1,0:T(8,128)(2,1)} %all-gather.3.cloned.1.call-done), kind=kOutput, calls=%fused_computation.2 | convolution fusion | flops 8606449664 | bytes 8929280 | tf_op jit(solution)/shard_map/rd,md->rm/dot_general | solution.py:25
  90.3 51.4 %all-gather.5.cloned.1.call-done = bf16[4096,1024]{1,0:T(8,128)(2,1)} async-done(((bf16[1024,1024]{1,0:T(8,128)(2,1)}), bf16[4096,1024]{1,0:T(8,128)(2,1)}) %all-gather.5.cloned.1.call-update) | async-done | bytes 8388624 | tf_op jit(solution)/shard_map/all_gather | solution.py:62
  141.8 28.4 %select_reduce_fusion = bf16[128,4096]{1,0:T(8,128)(2,1)S(1)} fusion(s32[4096]{0:T(1024)S(1)} %all_gather.14, s32[128,16]{1,0:T(8,128)S(1)} %bitcast.20, bf16[2048,1024]{1,0:T(8,128)(2,1)} %bitcast.18, bf16[4096,1024]{1,0:T(8,128)(2,1)} %all-gather.5.cloned.1.call-done), kind=kOutput, calls=%fused_computation | convolution fusion | flops 17212899328 | bytes 13656064 | tf_op jit(solution)/shard_map/rd,md->rm/dot_general | solution.py:25
  170.2 8.3 %convolution_convert_fusion = bf16[2048,4096]{1,0:T(8,128)(2,1)} fusion(bf16[128,2048]{1,0:T(8,128)(2,1)S(1)} %select_reduce_fusion.1, bf16[128,4096]{1,0:T(8,128)(2,1)S(1)} %select_reduce_fusion), kind=kOutput, calls=%fused_computation.4 | convolution fusion | flops 2155872256 | bytes 18350080 | tf_op jit(solution)/shard_map/dot_general | solution.py:73
  178.5 0.0 copy-start.3
  178.5 0.0 reduce-scatter.2.cloned.1.call-update
  178.5 0.7 copy-done.3
  179.2 0.1 reshape.39
  179.3 0.2 convolution_bitcast_fusion
  179.5 62.6 %psum.7 = f32[3,1024]{1,0:T(4,128)S(1)} all-reduce(f32[3,1024]{1,0:T(4,128)S(1)} %convolution_bitcast_fusion), channel_id=1, replica_groups=mesh['dp'=16,'row'=4,'col'=2] {'dp'}, use_global_device_ids=true, to_apply=%region_6.7 | all-reduce | flops 3072 | bytes 24576 | tf_op jit(solution)/shard_map/psum | solution.py:69
  242.1 0.6 broadcast_multiply_fusion
  242.7 46.3 %reduce-scatter.2.cloned.1.call-done = bf16[128,4096]{1,0:T(8,128)(2,1)} async-done(((bf16[2048,4096]{1,0:T(8,128)(2,1)}), bf16[128,4096]{1,0:T(8,128)(2,1)}) %reduce-scatter.2.cloned.1.call-update) | async-done | bytes 1048592 | tf_op jit(solution)/shard_map/reduce_scatter | solution.py:72
  289.0 1.4 convert_multiply_fusion.1
  290.5 2.4 reshape.38
  (4 shorter events, 0.1 us)
Async XLA Ops:
  7.2 6.7 %copy-start = (s32[2,64,32]{1,2,0:T(8,128)S(1)}, s32[2,64,32]{1,2,0:T(8,128)}, u32[]{:S(2)}) copy-start(s32[2,64,32]{1,2,0:T(8,128)} %param.8) | copy-start | bytes 49156
  7.2 6.8 %copy-start.2 = (s32[2,64,16]{1,2,0:T(8,128)S(1)}, s32[2,64,16]{1,2,0:T(8,128)}, u32[]{:S(2)}) copy-start(s32[2,64,16]{1,2,0:T(8,128)} %param.10) | copy-start | bytes 24580
  7.2 6.8 %copy-start.4 = (s32[2,64]{1,0:T(2,128)S(1)}, s32[2,64]{1,0:T(2,128)}, u32[]{:S(2)}) copy-start(s32[2,64]{1,0:T(2,128)} %param.9) | copy-start | bytes 1540
  7.2 6.9 %copy-start.1 = (s32[1024]{0:T(1024)S(1)}, s32[1024]{0:T(1024)}, u32[]{:S(2)}) copy-start(s32[1024]{0:T(1024)} %param.12) | copy-start | bytes 12292
  7.2 68.6 %all-gather.3.cloned.1.call-start = ((), (), s32[]{:S(2)}) async-start(), calls=%async_computation.1 | async-start | bytes 6291456 | tf_op jit(solution)/shard_map/all_gather | solution.py:56
  13.1 128.7 %all-gather.5.cloned.1.call-start = ((), (), s32[]{:S(2)}) async-start(), calls=%async_computation.2 | async-start | bytes 10485760 | tf_op jit(solution)/shard_map/all_gather | solution.py:62
  13.8 275.2 %reduce-scatter.2.cloned.1.call-start = ((), (), s32[]{:S(2)}) async-start(), calls=%async_computation.3 | async-start | bytes 17825792 | tf_op jit(solution)/shard_map/reduce_scatter | solution.py:72
  178.5 0.7 copy-start.3
Sparse Core Ops, SparseCore 0:
  13.2 62.5 all-gather.2
  78.0 63.7 all-gather.4
  178.7 110.3 reduce-scatter.1
where the time goes:
time: 300 us; the launch traced here: 299 us
  waiting for transfers between devices  139 us (46%)
  blocking collectives  74.8 us (25%)
  matrix products  57.1 us (19%)
  between operations  13.9 us (5%)
  other arithmetic  10.8 us (4%)
  local copies, waits for them, and re-layouts  3.34 us (1%)
    psum x1, blocking collectives, shards(): rhs = lax.psum(partial_rhs, 'dp') / total  62.6 us
    all_gather x1, waiting for transfers between devices, shards(): lax.all_gather(point_unit, 'row', axis=0, tiled=True)  51.4 us
    reduce_scatter x1, waiting for transfers between devices, shards(): lax.psum_scatter(lax.dot_general(row_kernel, col_kernel, contract, prefer...  46.3 us
    dot_general x2, matrix products, kernel_block(): jnp.einsum('rd,md->rm', bead_unit.reshape(config_rows * beads, width), po...  43 us
    all_gather x1, waiting for transfers between devices, shards(): lax.all_gather(point_unit, 'col', axis=0, tiled=True)  40.9 us
    all_gather x1, blocking collectives, shards(): lax.all_gather(sparse_type, 'row', axis=0, tiled=True)  8.4 us
    dot_general x1, matrix products, shards(): lax.dot_general(row_kernel, col_kernel, contract, preferred_element_type=...  8.31 us
    convert_element_type x2, other arithmetic, unit_rows(): return (widened / scale).astype(jnp.bfloat16)  6.26 us
  transfers between devices with their start and end apart: 3, of which 3 were waited for; matrix products, arithmetic and copies ran while one was open for 8% of the time, Pallas kernels for 0%

commit v1 on v0

--- a/solution.py
+++ b/solution.py
@@ -43,41 +43,26 @@
     live_type = jnp.where(slots[None, None, :] < bead_count[:, :, None], bead_type, -1).reshape(
         config_rows, beads
     )
-    point_unit = unit_rows(sparse_points)
     shard = sparse_points.shape[0]
-    total = config_rows * lax.axis_size("dp")
-
-    def place_kernel(parts):
-        block = kernel_block(units, live_type, parts[0], parts[1])
-        return block
-
-    row_kernel = place_kernel(
-        (
-            lax.all_gather(point_unit, "col", axis=0, tiled=True),
-            lax.all_gather(sparse_type, "col", axis=0, tiled=True),
-        )
-    ).astype(jnp.bfloat16)
-    col_kernel = place_kernel(
-        (
-            lax.all_gather(point_unit, "row", axis=0, tiled=True),
-            lax.all_gather(sparse_type, "row", axis=0, tiled=True),
-        )
-    ).astype(jnp.bfloat16)
-    own_kernel = lax.dynamic_slice_in_dim(row_kernel, lax.axis_index("col") * shard, shard, 1)
+    members = lax.axis_size("dp")
+    rows = lax.axis_size("row")
+    total = config_rows * members
+    own = kernel_block(units, live_type, unit_rows(sparse_points), sparse_type).astype(jnp.bfloat16)
+    columns = lax.all_gather(own, "dp", axis=0, tiled=True)
     weights = jnp.transpose(targets, (1, 0, 2)).reshape(3, config_rows)
-    partial_rhs = jnp.dot(weights, own_kernel.astype(jnp.float32), precision=lax.Precision.HIGHEST)
-    rhs = lax.psum(partial_rhs, "dp") / total
-    own_rows = row_kernel.shape[1] // lax.axis_size("dp")
-    contract = (((0,), (0,)), ((), ()))
-    gram_local = lax.psum_scatter(
-        lax.dot_general(
-            row_kernel, col_kernel, contract, preferred_element_type=jnp.float32
-        ).astype(jnp.bfloat16),
-        "dp",
-        scatter_dimension=0,
-        tiled=True,
-    ).astype(jnp.float32)
-    gram = (gram_local / total).reshape(own_rows, lax.axis_size("row"), shard)
+    weights = lax.all_gather(weights, "dp", axis=1, tiled=True)
+    rhs = jnp.dot(weights, columns.astype(jnp.float32), precision=lax.Precision.HIGHEST) / total
+    width_rows = shard * lax.axis_size("col") // members
+    strips_of = shard // width_rows
+    member = lax.axis_index("dp")
+    strip = lax.dynamic_slice_in_dim(columns, (member % strips_of) * width_rows, width_rows, 1)
+    strips = lax.all_gather(strip, ("row", "col"), axis=0, tiled=False)
+    strips = strips.reshape(rows, lax.axis_size("col"), total, width_rows)
+    strips = lax.dynamic_index_in_dim(strips, member // strips_of, 1, keepdims=False)
+    blocks = jnp.einsum("rni,nj->rij", strips, columns, preferred_element_type=jnp.float32)
+    blocks = (blocks / total).astype(jnp.bfloat16)
+    blocks = lax.all_to_all(blocks, "row", 0, 0, tiled=False)
+    gram = jnp.transpose(blocks, (1, 0, 2)).astype(jnp.float32)
     return (gram, rhs)
 
 

time: 300 us -> 204 us (0.68)
  blocking collectives: 74.8 us -> 19.6 us
  matrix products: 57.1 us -> 26.4 us
  waiting for transfers between devices: 139 us -> 124 us
  other arithmetic: 10.8 us -> 5.11 us
  starting transfers between devices: 0.12 us -> 5.42 us
    psum x1 -> x0, blocking collectives: 62.6 us -> none  [shards(): rhs = lax.psum(partial_rhs, 'dp') / total]
    reduce_scatter x1 -> x0, waiting for transfers between devices: 46.3 us -> none  [shards(): lax.psum_scatter(lax.dot_general(row_kernel, col_kernel, contract, prefer...]
    dot_general x2 -> x1, matrix products: 43 us -> 7.17 us  [kernel_block(): jnp.einsum('rd,md->rm', bead_unit.reshape(config_rows * beads, width), po...]
    all_gather x2, waiting for transfers between devices: 92.4 us -> 124 us  [the longest x1 69.3 us: shards(): strips = lax.all_gather(strip, ('row', 'col'), axis=0, tiled=False)]
    all_gather x2 -> x1, blocking collectives: 12.2 us -> 19.6 us  [shards(): weights = lax.all_gather(weights, 'dp', axis=1, tiled=True)]
    all_to_all x0 -> x1, starting transfers between devices: none -> 5.34 us  [shards(): blocks = lax.all_to_all(blocks, 'row', 0, 0, tiled=False)]
    convert_element_type x2 -> x1, other arithmetic: 6.26 us -> 4 us  [unit_rows(): return (widened / scale).astype(jnp.bfloat16)]
  transfers between devices with their start and end apart: 3 -> 3, of which waited for: 3 -> 2; matrix products, arithmetic and copies ran while one was open for 8% -> 2% of each run, Pallas kernels for 0% -> 0%
where the time goes in v1:
time: 204 us; the launch traced here: 201 us
  waiting for transfers between devices  124 us (61%)
  matrix products  26.4 us (13%)
  blocking collectives  19.6 us (10%)
  between operations  14.2 us (7%)
  local copies, waits for them, and re-layouts  5.58 us (3%)
  starting transfers between devices  5.42 us (3%)
  other arithmetic  5.11 us (3%)
    all_gather x1, waiting for transfers between devices, shards(): strips = lax.all_gather(strip, ('row', 'col'), axis=0, tiled=False)  69.3 us
    all_gather x1, waiting for transfers between devices, shards(): columns = lax.all_gather(own, 'dp', axis=0, tiled=True)  55 us
    all_gather x1, blocking collectives, shards(): weights = lax.all_gather(weights, 'dp', axis=1, tiled=True)  19.6 us
    dot_general x1, matrix products, bead_units(): jnp.einsum('sgba,sgad->sgbd', onehot, atom_feats, preferred_element_type=...  8.56 us
    dot_general x1, matrix products, kernel_block(): jnp.einsum('rd,md->rm', bead_unit.reshape(config_rows * beads, width), po...  7.17 us
    dot_general x1, matrix products, shards(): jnp.einsum('rni,nj->rij', strips, columns, preferred_element_type=jnp.flo...  6.15 us
    all_to_all x1, starting transfers between devices, shards(): blocks = lax.all_to_all(blocks, 'row', 0, 0, tiled=False)  5.34 us
    dot_general x1, matrix products, shards(): jnp.dot(weights, columns.astype(jnp.float32), precision=lax.Precision.HIG...  4.53 us
  transfers between devices with their start and end apart: 3, of which 2 were waited for; matrix products, arithmetic and copies ran while one was open for 2% of the time, Pallas kernels for 0%

profile of v1, /device:TPU:1, one launch (start us, length us, event | category | flops | bytes accessed | tf_op | source)
XLA Modules:
  0.0 200.6 jit_solution(10128126998354613125)
XLA Ops:
  7.2 0.0 all-gather.4.cloned.1.call-start
  7.2 0.8 copy.14
  8.1 0.3 convert_reduce_fusion
  8.4 0.0 copy-start.1
  8.4 0.0 copy-start.3
  8.4 0.0 copy-start
  8.5 8.6 %multiply_reduce_fusion = (f32[2,64,16]{2,1,0:T(8,128)S(1)}, f32[2,64,16,1024]{3,2,1,0:T(8,128)}) fusion(f32[2,64,16]{2,1,0:T(8,128)S(1)} %broadcast_maximum_fusion, bf16[2,64,32,1024]{3,2,1,0:T(8,128)(2,1)} %param.7, s32[2,64,32]{2,1,0:T(8,128)S(1)} %copy.14), kind=kOutput, calls=%fused_computation.3 | convolution fusion | flops 140572672 | bytes 16809984 | tf_op jit(solution)/shard_map/sgba,sgad->sgbd/dot_general | solution.py:18
  17.0 0.0 copy-done.1
  17.1 0.0 copy-done.3
  17.1 0.1 copy.17
  17.2 0.0 copy-done
  17.2 0.5 fusion
  17.7 0.0 copy-start.4
  17.7 4.0 %divide_convert_fusion = bf16[2,64,16,1024]{3,2,1,0:T(8,128)(2,1)S(1)} fusion(f32[2,64,16,1024]{3,2,1,0:T(8,128)} %get-tuple-element.7, f32[2,64,16]{2,1,0:T(8,128)S(1)} %sqrt_multiply_fusion), kind=kLoop, calls=%fused_computation.2 | loop fusion | flops 4194304 | bytes 12591104 | tf_op jit(solution)/shard_map/convert_element_type | solution.py:12
  21.7 0.0 copy-done.4
  21.7 7.2 %select_reduce_fusion = bf16[128,1024]{1,0:T(8,128)(2,1)} fusion(s32[1024]{0:T(1024)S(1)} %copy-done.4, s32[128,16]{1,0:T(8,128)S(1)} %bitcast.26, bf16[2048,1024]{1,0:T(8,128)(2,1)S(1)} %bitcast.25, bf16[1024,1024]{1,0:T(8,128)(2,1)S(1)} %copy-done, f32[1024]{0:T(1024)S(1)} %add_sqrt_fusion), kind=kOutput, calls=%fused_computation | convolution fusion | flops 4306370560 | bytes 6569984 | tf_op jit(solution)/shard_map/rd,md->rm/dot_general | solution.py:25
  28.9 0.0 all-gather.4.cloned.1.call-update
  28.9 0.0 all-gather.6.cloned.1.call-start
  29.0 55.0 %all-gather.4.cloned.1.call-done = bf16[2048,1024]{1,0:T(8,128)(2,1)} async-done(((bf16[128,1024]{1,0:T(8,128)(2,1)}), bf16[2048,1024]{1,0:T(8,128)(2,1)}) %all-gather.4.cloned.1.call-update) | async-done | bytes 4194320 | tf_op jit(solution)/shard_map/all_gather | solution.py:51
  83.9 1.9 constant_dynamic-slice_fusion
  85.8 0.0 all-gather.6.cloned.1.call-update
  85.8 69.3 %all-gather.6.cloned.1.call-done = bf16[16384,128]{1,0:T(8,128)(2,1)} async-done(((bf16[2048,128]{1,0:T(8,128)(2,1)}), bf16[16384,128]{1,0:T(8,128)(2,1)}) %all-gather.6.cloned.1.call-update) | async-done | bytes 4194320 | tf_op jit(solution)/shard_map/all_gather | solution.py:59
  155.1 0.0 copy-start.2
  155.1 6.2 %multiply_convert_fusion = bf16[4,128,1024]{2,1,0:T(8,128)(2,1)} fusion(bf16[2048,1024]{1,0:T(8,128)(2,1)} %all-gather.4.cloned.1.call-done, bf16[4,2,2048,128]{3,2,1,0:T(8,128)(2,1)} %bitcast.28, s32[]{:T(128)S(6)} %select_n.31), kind=kOutput, calls=%fused_computation.12 | convolution fusion | flops 2148532224 | bytes 7340036 | tf_op jit(solution)/shard_map/rni,nj->rij/dot_general | solution.py:62
  161.2 5.3 %all-to-all-start = ((bf16[4,128,1024]{2,1,0:T(8,128)(2,1)}), bf16[4,128,1024]{2,1,0:T(8,128)(2,1)S(1)}, u32[]{:S(2)}, u32[]{:S(2)}) async-start(bf16[4,128,1024]{2,1,0:T(8,128)(2,1)} %multiply_convert_fusion), calls=%async_computation | async-start | bytes 2097152 | tf_op jit(solution)/shard_map/all_to_all | solution.py:64
  166.6 0.0 copy-done.2
  166.6 0.1 reshape.36
  166.7 19.6 %all_gather.15 = f32[3,2048]{1,0:T(4,128)S(1)} all-gather(f32[3,128]{1,0:T(4,128)S(1)} %reshape.36), channel_id=1, replica_groups=mesh['dp'=16,'row'=4,'col'=2] {'dp'}, dimensions={1}, use_global_device_ids=true | all-gather | bytes 26112 | tf_op jit(solution)/shard_map/all_gather | solution.py:53
  186.3 4.5 %fusion.12 = f32[3,1024]{1,0:T(4,128)} fusion(bf16[2048,1024]{1,0:T(8,128)(2,1)} %all-gather.4.cloned.1.call-done, f32[3,2048]{1,0:T(4,128)S(1)} %all_gather.15), kind=kOutput, calls=%fused_computation.16 | convolution fusion | flops 75500544 | bytes 4231168 | tf_op jit(solution)/shard_map/dot_general | solution.py:54
  190.8 0.0 all-to-all-done
  190.8 0.2 convert_bitcast_fusion
  191.1 2.7 %copy.16 = f32[128,4,1024]{2,1,0:T(4,128)} copy(f32[128,4,1024]{2,0,1:T(8,128)S(1)} %convert_bitcast_fusion) | data formatting | bytes 4194304
  (4 shorter events, 0.1 us)
Async XLA Ops:
  7.2 76.8 %all-gather.4.cloned.1.call-start = ((), (), s32[]{:S(2)}) async-start(), calls=%async_computation.1 | async-start | bytes 4456448 | tf_op jit(solution)/shard_map/all_gather | solution.py:51
  8.4 8.6 %copy-start.1 = (s32[2,64,16]{1,2,0:T(8,128)S(1)}, s32[2,64,16]{1,2,0:T(8,128)}, u32[]{:S(2)}) copy-start(s32[2,64,16]{1,2,0:T(8,128)} %param.10) | copy-start | bytes 24580
  8.4 8.6 %copy-start.3 = (s32[2,64]{1,0:T(2,128)S(1)}, s32[2,64]{1,0:T(2,128)}, u32[]{:S(2)}) copy-start(s32[2,64]{1,0:T(2,128)} %param.9) | copy-start | bytes 1540
  8.4 8.7 %copy-start = (bf16[1024,1024]{1,0:T(8,128)(2,1)S(1)}, bf16[1024,1024]{1,0:T(8,128)(2,1)}, u32[]{:S(2)}) copy-start(bf16[1024,1024]{1,0:T(8,128)(2,1)} %param.11) | copy-start | bytes 6291460
  17.7 4.0 %copy-start.4 = (s32[1024]{0:T(1024)S(1)}, s32[1024]{0:T(1024)}, u32[]{:S(2)}) copy-start(s32[1024]{0:T(1024)} %param.12) | copy-start | bytes 12292
  28.9 126.2 %all-gather.6.cloned.1.call-start = ((), (), s32[]{:S(2)}) async-start(), calls=%async_computation.2 | async-start | bytes 4718592 | tf_op jit(solution)/shard_map/all_gather | solution.py:59
  155.1 11.5 %copy-start.2 = (f32[2,3,64]{2,0,1:T(2,128)S(1)}, f32[2,3,64]{2,0,1:T(2,128)}, u32[]{:S(2)}) copy-start(f32[2,3,64]{2,0,1:T(2,128)} %param.13) | copy-start | bytes 4612
  161.2 29.6 %all-to-all-start = ((bf16[4,128,1024]{2,1,0:T(8,128)(2,1)}), bf16[4,128,1024]{2,1,0:T(8,128)(2,1)S(1)}, u32[]{:S(2)}, u32[]{:S(2)}) async-start(bf16[4,128,1024]{2,1,0:T(8,128)(2,1)} %multiply_convert_fusion), calls=%async_computation | async-start | bytes 2097152 | tf_op jit(solution)/shard_map/all_to_all | solution.py:64
Sparse Core Ops, SparseCore 0:
  29.0 54.8 all-gather.3
  86.1 68.9 all-gather.5

commit v2 on v1

v2 whole, which is shorter than its diff:
```python
import functools

import jax
import jax.numpy as jnp
from jax import lax
from jax.experimental import pallas as pl
from jax.experimental.pallas import tpu as pltpu
from jax.sharding import PartitionSpec as P

EPSILON = 1e-06
MESH = pl.DeviceIdType.MESH
LOG2E = 1.4426950408889634

SIDE = 4
GROUP = 8
SUB = 32
HALF = 2 * SUB
STRIP = 128


def kernel(
    total,
    atoms_hbm, points_hbm, key_ref, live_ref, ptype_ref, weight_ref,
    gram_out, rhs_out,
    atoms, points, units, kbuf, sbuf, wbuf, acc, obuf,
    load_sem, k_send, k_recv, s_send, s_recv, w_send, w_recv, o_send, o_recv, o_local,
):
    width = points.shape[1]
    shard = points.shape[0]
    beads = units.shape[0] // SUB
    slots = beads * GROUP
    dp = lax.axis_index("dp")
    row = lax.axis_index("row")
    col = lax.axis_index("col")
    x, z = dp // SIDE, dp % SIDE
    h, core = row // 2, row % 2
    y = h * 2 + col
    at_strip = dp % 8
    owner = (dp // 8) == col

    def on_x(step):
        return {"dp": ((x + step) % SIDE) * SIDE + z, "row": row, "col": col}

    def on_z(step):
        return {"dp": x * SIDE + (z + step) % SIDE, "row": row, "col": col}

    def on_y(step, at_core):
        to = (y + step) % SIDE
        return {"dp": dp, "row": (to // 2) * 2 + at_core, "col": to % 2}

    sibling = on_y(0, 1 - core)
    up, down = on_y(1, core), on_y(-1, core)
    h_up, h_down = ((y + 1) % SIDE) // 2, ((y - 1) % SIDE) // 2

    loads = []
    order = (0, 2, 1, 3)
    per_sub = SUB // GROUP
    load_points = pltpu.make_async_copy(points_hbm, points, load_sem.at[4])
    load_points.start()
    for t in order:
        rows = pl.ds(t * per_sub, per_sub)
        copy = pltpu.make_async_copy(atoms_hbm.at[rows], atoms.at[rows], load_sem.at[t])
        copy.start()
        loads.append(copy)

    barrier = pltpu.get_barrier_semaphore()
    peers = [on_x(1), on_x(2), on_x(3), on_z(1), on_z(2), on_z(3), sibling, up, down]
    peers += [on_y(2, core), on_y(2, 1 - core)]
    for peer in peers:
        pl.semaphore_signal(barrier, inc=1, device_id=peer, device_id_type=MESH)

    wbuf[0, 0] = weight_ref[...]

    pending = []

    def remote(src, dst, send, recv, peer):
        return pltpu.make_async_remote_copy(
            src_ref=src, dst_ref=dst, send_sem=send, recv_sem=recv,
            device_id=peer, device_id_type=MESH,
        )

    def slot(route, outer, inner, sub):
        return kbuf.at[route, outer % SIDE, pl.ds((inner % SIDE) * HALF + sub * SUB, SUB), :]

    def recv_sem(route, outer, inner, sub):
        return k_recv.at[((route * SIDE + outer % SIDE) * SIDE + inner % SIDE) * 2 + sub]

    def along(route, phase, step):
        return on_x(step) if (route == 0) == (phase == 0) else on_z(step)

    def send(route, outer, inner, sub, phase, step):
        if phase == 0:
            to = (route, outer, inner - step, sub)
        else:
            to = (route, outer - step, inner, sub)
        copy = remote(
            slot(route, outer, inner, sub), slot(*to), k_send.at[len(pending)], recv_sem(*to),
            along(route, phase, step),
        )
        copy.start()
        pending.append(copy)

    def arrived(route, outer, inner, sub):
        here = slot(route, outer, inner, sub)
        remote(here, here, k_send.at[0], recv_sem(route, outer, inner, sub), sibling).wait_recv()

    def send_own(route, sub):
        for step in (1, -1):
            send(route, 0, 0, sub, 0, step)
        for step in (1, -1):
            send(route, 0, 0, sub, 1, step)

    def inner_step(route, inner, sub):
        arrived(route, 0, inner, sub)
        if inner == 3 and sub == 0:
            send(route, 0, inner, sub, 0, 1)
        if inner == 1 and sub == 1:
            send(route, 0, inner, sub, 0, -1)
        for step in (1, -1):
            send(route, 0, inner, sub, 1, step)

    def outer_step(route, inner):
        arrived(route, 3, inner, 0)
        send(route, 3, inner, 0, 1, 1)
        arrived(route, 1, inner, 1)
        send(route, 1, inner, 1, 1, -1)

    row_id = lax.broadcasted_iota(jnp.int32, (slots, GROUP * 32), 0)

    def unit_points():
        def body(i, carry):
            rows = pl.ds(pl.multiple_of(i * 128, 128), 128)
            wide = points[rows, :].astype(jnp.float32)
            mean = jnp.sum(wide * wide, axis=1, keepdims=True) * (1.0 / width)
            points[rows, :] = (wide * lax.rsqrt(mean + EPSILON)).astype(jnp.bfloat16)
            return carry
        lax.fori_loop(0, shard // 128, body, 0)

    def unit_beads(t):
        for i in range(per_sub):
            j = t * per_sub + i
            onehot = jnp.where(key_ref[j:j + 1, :] == row_id, 1.0, 0.0)
            size = jnp.maximum(jnp.sum(onehot, axis=1, keepdims=True), 1.0)
            summed = jnp.dot(onehot.astype(jnp.bfloat16), atoms[j], preferred_element_type=jnp.float32)
            inverse = 1.0 / size
            mean = jnp.sum(summed * summed, axis=1, keepdims=True) * (inverse * inverse * (1.0 / width))
            scale = inverse * lax.rsqrt(mean + EPSILON)
            units[i * slots:(i + 1) * slots, :] = (summed * scale).astype(jnp.bfloat16)

    def kernel_rows(t):
        route, sub = t // 2, t % 2
        tile = 256

        def body(ct, carry):
            cols = pl.ds(pl.multiple_of(ct * tile, tile), tile)
            scores = lax.dot_general(
                units[...], points[cols, :], (((1,), (1,)), ((), ())),
                preferred_element_type=jnp.float32,
            )
            kind = ptype_ref[:, cols]
            parts = []
            for i in range(per_sub):
                j = t * per_sub + i
                part = jnp.exp2(scores[i * slots:(i + 1) * slots] * (LOG2E * width ** (-0.5)))
                part = jnp.where(live_ref[:, j:j + 1] == kind, part, 0.0)
                parts.append(jnp.sum(part.reshape(beads, GROUP, tile), axis=0))
            kbuf[route, 0, sub * SUB:(sub + 1) * SUB, cols] = jnp.concatenate(parts, axis=0).astype(jnp.bfloat16)
            return carry
        lax.fori_loop(0, shard // tile, body, 0)

    groups = [(route, outer) for outer in (0, 3, 1, 2) for route in (0, 1)]
    index_of = {group: g for g, group in enumerate(groups)}

    def strip(g, r):
        return sbuf.at[g, pl.ds(pl.multiple_of(r * STRIP, STRIP), STRIP), :]

    def strip_copy(g, r, which, peer):
        here = strip(g, r)
        return remote(here, here, s_send.at[g * 4 + which], s_recv.at[g * 4 + r], peer)

    def strip_arrived(g, r):
        strip_copy(g, r, 0, sibling).wait_recv()

    def strip_send(group):
        g = index_of[group]

        @pl.when(owner)
        def _():
            route, outer = group
            lanes = pl.ds(pl.multiple_of(at_strip * STRIP, STRIP), STRIP)
            mine = kbuf[route, outer, :, lanes]
            sbuf[g, pl.ds(pl.multiple_of(row * STRIP, STRIP), STRIP), :] = mine.T
            strip_copy(g, row, 0, up).start()
            strip_copy(g, row, 1, down).start()
            strip_copy(g, row, 2, sibling).start()

    def strip_relay(group):
        g = index_of[group]
        other = (1 - h) * 2 + core
        r_up, r_down = h_up * 2 + core, h_down * 2 + core

        @pl.when(jnp.logical_not(owner))
        def _():
            strip_arrived(g, r_down)
            strip_copy(g, r_down, 0, sibling).start()
            strip_arrived(g, r_up)
            strip_copy(g, r_up, 1, sibling).start()

            @pl.when(h == g % 2)
            def _():
                strip_copy(g, r_down, 2, up).start()
                strip_copy(g, r_up, 3, down).start()

        @pl.when(owner)
        def _():
            strip_arrived(g, other)
            strip_copy(g, other, 3, sibling).start()

    def strip_drain(group):
        g = index_of[group]
        for which in range(2):
            strip_copy(g, row, which, sibling).wait_send()

        @pl.when(jnp.logical_or(owner, h == g % 2))
        def _():
            for which in range(2, 4):
                strip_copy(g, row, which, sibling).wait_send()

    def strips_here(group):
        g = index_of[group]
        strip_arrived(g, 1 - core)
        strip_arrived(g, 2 + 1 - core)

    def gram(group, first=False):
        g = index_of[group]
        strips_here(group)
        route, outer = group
        tile = 256

        def body(ct, carry):
            cols = pl.ds(pl.multiple_of(ct * tile, tile), tile)
            part = jnp.dot(sbuf[g], kbuf[route, outer, :, cols], preferred_element_type=jnp.float32)
            if first:
                acc[:, cols] = part
            else:
                acc[:, cols] += part
            return carry
        lax.fori_loop(0, shard // tile, body, 0)

    def weight_copy(axis, step):
        if axis == 0:
            src, dst, peer = wbuf.at[0, 0], wbuf.at[0, (-step) % SIDE], on_x(step)
        else:
            src, dst, peer = wbuf.at[0], wbuf.at[(-step) % SIDE], on_z(step)
        i = axis * 3 + step - 1
        return remote(src, dst, w_send.at[i], w_recv.at[i], peer)

    def weight_rows():
        low = lax.broadcasted_iota(jnp.int32, (8, 128), 1) < HALF
        for (route, outer), g in index_of.items():
            if route == 0:
                parts = [wbuf[outer, i] for i in range(SIDE)]
                pairs = [jnp.where(low, parts[i], pltpu.roll(parts[i + 1], HALF, 1)) for i in (0, 2)]
            else:
                parts = [wbuf[i, outer] for i in range(SIDE)]
                pairs = [jnp.where(low, pltpu.roll(parts[i], HALF, 1), parts[i + 1]) for i in (0, 2)]
            wide = jnp.concatenate(pairs, axis=1)
            high = wide.astype(jnp.bfloat16).astype(jnp.float32)
            both = jnp.concatenate([high, wide - high], axis=0)
            sbuf[g, 4 * STRIP:, :] = both.astype(jnp.bfloat16)

    load_points.wait()
    unit_points()
    loads[0].wait()
    unit_beads(0)
    kernel_rows(0)
    pl.semaphore_wait(barrier, len(peers))
    send_own(0, 0)
    for step in (1, 2, 3):
        weight_copy(0, step).start()
    loads[1].wait()
    unit_beads(2)
    kernel_rows(2)
    send_own(1, 0)
    loads[2].wait()
    unit_beads(1)
    kernel_rows(1)
    send_own(0, 1)
    inner_step(0, 3, 0)
    inner_step(0, 1, 0)
    for step in (1, 2, 3):
        weight_copy(0, step).wait_recv()
    for step in (1, 2, 3):
        weight_copy(1, step).start()
    loads[3].wait()
    unit_beads(3)
    kernel_rows(3)
    send_own(1, 1)
    inner_step(1, 3, 0)
    inner_step(1, 1, 0)
    for route in (0, 1):
        inner_step(route, 1, 1)
        inner_step(route, 3, 1)
    for route in (0, 1):
        outer_step(route, 0)
    for route in (0, 1):
        inner_step(route, 2, 0)
        inner_step(route, 2, 1)
    strip_send((0, 0))
    strip_send((1, 0))
    for route in (0, 1):
        outer_step(route, 3)
    for step in (1, 2, 3):
        weight_copy(1, step).wait_recv()
    weight_rows()
    strip_relay((0, 0))
    strip_relay((1, 0))
    for route in (0, 1):
        outer_step(route, 1)
    gram((0, 0), first=True)
    gram((1, 0))
    for route in (0, 1):
        outer_step(route, 2)
    for outer, sub in ((3, 1), (1, 0)):
        for route in (0, 1):
            for inner in range(SIDE):
                arrived(route, outer, inner, sub)
            strip_send((route, outer))
    for outer in (3, 1):
        for route in (0, 1):
            strip_relay((route, outer))
    for outer in (3, 1):
        for route in (0, 1):
            gram((route, outer))
    for route in (0, 1):
        for inner in (0, 3, 1, 2):
            for sub in (0, 1):
                arrived(route, 2, inner, sub)
        strip_send((route, 2))
    for route in (0, 1):
        strip_relay((route, 2))
    for route in (0, 1):
        strips_here((route, 2))

    def finish(rows, cols):
        value = acc[rows, cols]
        for route in (0, 1):
            g = index_of[(route, 2)]
            value += jnp.dot(sbuf[g, rows, :], kbuf[route, 2, :, cols], preferred_element_type=jnp.float32)
        return value * (1.0 / total)

    def block(r):
        rows = pl.ds(pl.multiple_of(r * STRIP, STRIP), STRIP)
        obuf[r] = finish(rows, pl.ds(0, shard)).astype(jnp.bfloat16)

    def out_copy(r, which, peer):
        return remote(obuf.at[r], gram_out.at[row], o_send.at[which], o_recv.at[r], peer)

    far = (1 - h) * 2
    targets = [
        (far + core, on_y(2, core)), (far + 1 - core, on_y(2, 1 - core)), (h * 2 + 1 - core, sibling),
    ]
    for which, (r, peer) in enumerate(targets):
        block(r)
        remote(obuf.at[r], gram_out.at[row], o_send.at[which], o_recv.at[row], peer).start()
    block(row)
    keep = pltpu.make_async_copy(obuf.at[row], gram_out.at[row], o_local)
    keep.start()
    tail = finish(pl.ds(4 * STRIP, 16), pl.ds(0, shard))
    rhs_out[...] = tail[0:3] + tail[8:11]
    for copy in pending:
        copy.wait_send()
    for group in groups:
        strip_drain(group)
    for axis in (0, 1):
        for step in (1, 2, 3):
            weight_copy(axis, step).wait_send()
    keep.wait()
    for which, (r, peer) in enumerate(targets):
        copy = remote(obuf.at[r], gram_out.at[r], o_send.at[which], o_recv.at[r], peer)
        copy.wait_send()
        copy.wait_recv()


def shards(atom_feats, atom_bead, bead_count, bead_type, sparse_points, sparse_type, targets):
    slabs, local, atoms, width = atom_feats.shape
    beads = bead_type.shape[-1]
    config_rows = slabs * local
    shard = sparse_points.shape[0]
    total = config_rows * lax.axis_size("dp")
    blocks = config_rows // GROUP
    place = jnp.arange(GROUP * atoms, dtype=jnp.int32)[None, :] // atoms
    key = atom_bead.reshape(blocks, GROUP * atoms) * GROUP + place
    slots = jnp.arange(beads, dtype=jnp.int32)
    live = jnp.where(slots[None, None, :] < bead_count[:, :, None], bead_type, -1)
    live = jnp.transpose(live.reshape(blocks, GROUP, beads), (2, 1, 0)).reshape(beads * GROUP, blocks)
    weights = jnp.transpose(targets, (1, 0, 2)).reshape(3, config_rows)
    weights = jnp.pad(weights, ((0, 5), (0, 0)))
    bf16, f32 = jnp.bfloat16, jnp.float32
    dma = pltpu.SemaphoreType.DMA
    vmem = pl.BlockSpec(memory_space=pltpu.VMEM)
    hbm = pl.BlockSpec(memory_space=pl.ANY)
    gram, rhs = pl.pallas_call(
        functools.partial(kernel, total),
        out_shape=(
            jax.ShapeDtypeStruct((4, STRIP, shard), bf16),
            jax.ShapeDtypeStruct((3, shard), f32),
        ),
        in_specs=[hbm, hbm, vmem, vmem, vmem, vmem],
        out_specs=(hbm, vmem),
        scratch_shapes=[
            pltpu.VMEM((blocks, GROUP * atoms, width), bf16),
            pltpu.VMEM((shard, width), bf16),
            pltpu.VMEM((SUB * beads, width), bf16),
            pltpu.VMEM((2, SIDE, SIDE * HALF, shard), bf16),
            pltpu.VMEM((8, 4 * STRIP + 16, SIDE * HALF), bf16),
            pltpu.VMEM((SIDE, SIDE, 8, 128), f32),
            pltpu.VMEM((4 * STRIP + 16, shard), f32),
            pltpu.VMEM((4, STRIP, shard), bf16),
            dma((5,)),
            dma((60,)),
            dma((64,)),
            dma((32,)),
            dma((32,)),
            dma((6,)),
            dma((6,)),
            dma((3,)),
            dma((4,)),
            dma,
        ],
        compiler_params=pltpu.CompilerParams(
            collective_id=0, has_side_effects=True, vmem_limit_bytes=44 * 1024 * 1024
        ),
    )(
        atom_feats.reshape(blocks, GROUP * atoms, width), sparse_points, key, live,
        sparse_type.reshape(1, shard), weights,
    )
    return (jnp.transpose(gram, (1, 0, 2)).astype(jnp.float32), rhs)


def solution(mesh):
    return jax.shard_map(
        shards,
        mesh=mesh,
        in_specs=(
            P(None, "dp", None, None),
            P(None, "dp", None),
            P(None, "dp"),
            P(None, "dp", None),
            P(("row", "col"), None),
            P(("row", "col")),
            P(None, None, "dp"),
        ),
        out_specs=(P(("row", "dp"), None, "col"), P(None, ("row", "col"))),
        check_vma=False,
    )
```

time: 204 us -> 87 us (0.43); the launches traced: 201 us -> 86.7 us
  waiting for transfers between devices: 124 us -> 0 us
  Pallas kernels: 0 us -> 76.9 us
  matrix products: 26.4 us -> 0 us
  blocking collectives: 19.6 us -> 0 us
  between operations: 14.2 us -> 0.69 us
  starting transfers between devices: 5.42 us -> 0 us
  other arithmetic: 5.11 us -> 1.76 us
    all_gather x2 -> x0, waiting for transfers between devices: 124 us -> none  [the longest x1 69.3 us: shards(): strips = lax.all_gather(strip, ('row', 'col'), axis=0, tiled=False)]
    pallas_call x0 -> x1, Pallas kernels: none -> 76.9 us  [shards(): pl.pallas_call(functools.partial(kernel, total), out_shape=(jax.ShapeDtyp...]
    dot_general x4 -> x0, matrix products: 26.4 us -> none  [the longest x1 8.56 us: bead_units(): jnp.einsum('sgba,sgad->sgbd', onehot, atom_feats, preferred_element_type=...]
    all_gather x1 -> x0, blocking collectives: 19.6 us -> none  [shards(): weights = lax.all_gather(weights, 'dp', axis=1, tiled=True)]
    all_to_all x1 -> x0, starting transfers between devices: 5.34 us -> none  [shards(): blocks = lax.all_to_all(blocks, 'row', 0, 0, tiled=False)]
    convert_element_type x2 -> x1, other arithmetic: 4.24 us -> 0.24 us  [shards(): return (jnp.transpose(gram, (1, 0, 2)).astype(jnp.float32), rhs)]
    unnamed x12 -> x7, local copies, waits for them, and re-layouts: 3.54 us -> 6.35 us
  transfers between devices with their start and end apart: 3 -> 0, of which waited for: 2 -> 0; matrix products, arithmetic and copies ran while one was open for 2% -> 0% of each run, Pallas kernels for 0% -> 0%
where the time goes in v2:
time: 87 us; the launch traced here: 86.7 us
  Pallas kernels  76.9 us (88%)
  local copies, waits for them, and re-layouts  7.39 us (8%)
  other arithmetic  1.76 us (2%)
    pallas_call x1, Pallas kernels, shards(): pl.pallas_call(functools.partial(kernel, total), out_shape=(jax.ShapeDtyp...  76.9 us
    unnamed x7, local copies, waits for them, and re-layouts  6.35 us

profile of v2, /device:TPU:1, one launch (start us, length us, event | category | flops | bytes accessed | tf_op | source)
XLA Modules:
  0.0 86.7 jit_solution(3783417593985759241)
XLA Ops:
  0.6 0.8 reshape.64
  1.4 0.8 broadcast_multiply_fusion
  2.2 0.1 copy.11
  2.3 0.1 mul.11
  2.4 0.8 copy.12
  3.2 0.8 fusion
  3.9 0.1 copy.13
  4.0 0.0 copy-start
  4.0 1.6 %copy-done = bf16[1024,1024]{1,0:T(8,128)(2,1)S(1)} copy-done((bf16[1024,1024]{1,0:T(8,128)(2,1)S(1)}, bf16[1024,1024]{1,0:T(8,128)(2,1)}, u32[]{:S(2)}) %copy-start) | copy-done | bytes 2097176
  5.6 0.0 copy-start.1
  5.6 0.7 copy-done.1
  6.3 76.9 %shard_map.86 = (bf16[4,128,1024]{2,1,0:T(8,128)(2,1)S(1)}, f32[3,1024]{1,0:T(4,128)S(1)}) custom-call(bf16[16,256,1024]{2,1,0:T(8,128)(2,1)} %bitcast.11, bf16[1024,1024]{1,0:T(8,128)(2,1)S(1)} %copy-done, s32[16,256]{1,0:T(8,128)S(1)} %broadcast_add_fusion.key_ref, s32[128,16]{1,0:T(8,128)S(1)} %bitcast.9, s32[1,1024]{1,0:T(1,128)S(1)} %bitcast.10, ...), custom_call_target="tpu_custom_call" | custom-call | tf_op jit(solution)/shard_map/pallas_call | solution.py:403
  83.2 0.2 convert_bitcast_fusion
  83.4 2.7 %copy.14 = f32[128,4,1024]{2,1,0:T(4,128)} copy(f32[128,4,1024]{2,0,1:T(8,128)S(1)} %convert_bitcast_fusion) | data formatting | bytes 4194304
  86.1 0.6 copy.16
  (3 shorter events, 0.0 us)
Async XLA Ops:
  4.0 1.6 %copy-start = (bf16[1024,1024]{1,0:T(8,128)(2,1)S(1)}, bf16[1024,1024]{1,0:T(8,128)(2,1)}, u32[]{:S(2)}) copy-start(bf16[1024,1024]{1,0:T(8,128)(2,1)} %points_hbm.1) | copy-start | bytes 6291460
  5.6 0.7 copy-start.1

commit v3 on v2

--- a/solution.py
+++ b/solution.py
@@ -16,19 +16,21 @@
 SUB = 32
 HALF = 2 * SUB
 STRIP = 128
+ATOMS = 32
+BEADS = 16
 
 
 def kernel(
     total,
-    atoms_hbm, points_hbm, key_ref, live_ref, ptype_ref, weight_ref,
+    atoms_hbm, points_hbm, bead_hbm, count_hbm, type_hbm, ptype_hbm, targets_hbm,
     gram_out, rhs_out,
-    atoms, points, units, kbuf, sbuf, wbuf, acc, obuf,
-    load_sem, k_send, k_recv, s_send, s_recv, w_send, w_recv, o_send, o_recv, o_local,
+    atoms, points, units, kbuf, rbuf, sbuf, wbuf, acc, obuf,
+    bead_in, count_in, type_in, ptype, targets_in, repeated, live,
+    load_sem, k_send, k_recv, d_send, d_recv, s_send, s_recv, w_send, w_recv, o_send, o_recv, o_local,
 ):
     width = points.shape[1]
     shard = points.shape[0]
-    beads = units.shape[0] // SUB
-    slots = beads * GROUP
+    slots = BEADS * GROUP
     dp = lax.axis_index("dp")
     row = lax.axis_index("row")
     col = lax.axis_index("col")
@@ -38,11 +40,14 @@
     at_strip = dp % 8
     owner = (dp // 8) == col
 
+    def on_plane(step_x, step_z):
+        return {"dp": ((x + step_x) % SIDE) * SIDE + (z + step_z) % SIDE, "row": row, "col": col}
+
     def on_x(step):
-        return {"dp": ((x + step) % SIDE) * SIDE + z, "row": row, "col": col}
+        return on_plane(step, 0)
 
     def on_z(step):
-        return {"dp": x * SIDE + (z + step) % SIDE, "row": row, "col": col}
+        return on_plane(0, step)
 
     def on_y(step, at_core):
         to = (y + step) % SIDE
@@ -51,10 +56,19 @@
     sibling = on_y(0, 1 - core)
     up, down = on_y(1, core), on_y(-1, core)
     h_up, h_down = ((y + 1) % SIDE) // 2, ((y - 1) % SIDE) // 2
+    offsets = [(i, j) for i in range(SIDE) for j in range(SIDE) if (i, j) != (0, 0)]
 
     loads = []
-    order = (0, 2, 1, 3)
+    compute_order = order = (0, 2, 1, 3)
     per_sub = SUB // GROUP
+    small = []
+    for i, (src, dst) in enumerate((
+        (bead_hbm, bead_in), (count_hbm, count_in), (type_hbm, type_in), (ptype_hbm, ptype),
+        (targets_hbm, targets_in),
+    )):
+        copy = pltpu.make_async_copy(src, dst, load_sem.at[5 + i])
+        copy.start()
+        small.append(copy)
     load_points = pltpu.make_async_copy(points_hbm, points, load_sem.at[4])
     load_points.start()
     for t in order:
@@ -64,12 +78,10 @@
         loads.append(copy)
 
     barrier = pltpu.get_barrier_semaphore()
-    peers = [on_x(1), on_x(2), on_x(3), on_z(1), on_z(2), on_z(3), sibling, up, down]
-    peers += [on_y(2, core), on_y(2, 1 - core)]
+    peers = [on_plane(*offset) for offset in offsets]
+    peers += [sibling, up, down, on_y(2, core), on_y(2, 1 - core)]
     for peer in peers:
         pl.semaphore_signal(barrier, inc=1, device_id=peer, device_id_type=MESH)
-
-    wbuf[0, 0] = weight_ref[...]
 
     pending = []
 
@@ -119,13 +131,58 @@
         for step in (1, -1):
             send(route, 0, inner, sub, 1, step)
 
-    def outer_step(route, inner):
-        arrived(route, 3, inner, 0)
-        send(route, 3, inner, 0, 1, 1)
-        arrived(route, 1, inner, 1)
-        send(route, 1, inner, 1, 1, -1)
-
-    row_id = lax.broadcasted_iota(jnp.int32, (slots, GROUP * 32), 0)
+    def outer_step(route, inner, sub):
+        if sub == 0:
+            arrived(route, 3, inner, 0)
+            send(route, 3, inner, 0, 1, 1)
+        else:
+            arrived(route, 1, inner, 1)
+            send(route, 1, inner, 1, 1, -1)
+
+    def near(route, sub):
+        for inner in (3, 1) if sub == 0 else (1, 3):
+            inner_step(route, inner, sub)
+        outer_step(route, 0, sub)
+
+    def middle(route, sub):
+        inner_step(route, 2, sub)
+        outer_step(route, 3, sub)
+        outer_step(route, 1, sub)
+
+    def far(route, sub):
+        outer_step(route, 2, sub)
+
+    def prepare():
+        for copy in small:
+            copy.wait()
+        wbuf[0, 0] = jnp.zeros_like(wbuf[0, 0])
+        wbuf[0, 0, 0:3, :] = jnp.concatenate([targets_in[:, 0], targets_in[:, 1]], axis=1)
+        spread = lax.broadcasted_iota(jnp.int32, (ATOMS, 128), 1) % ATOMS
+        spread = jnp.where(spread == lax.broadcasted_iota(jnp.int32, (ATOMS, 128), 0), 1.0, 0.0)
+        for s in range(2):
+            here = slice(s * HALF, (s + 1) * HALF)
+            beads = bead_in[s].astype(jnp.float32).astype(jnp.bfloat16)
+            repeated[here, :] = lax.dot_general(
+                beads, spread.astype(jnp.bfloat16), (((0,), (0,)), ((), ())), preferred_element_type=jnp.float32
+            )
+            alive = lax.broadcasted_iota(jnp.int32, (BEADS, HALF), 0) < count_in[s:s + 1, :]
+            kinds = jnp.where(alive, type_in[s], -1).astype(jnp.float32).astype(jnp.bfloat16)
+            same = lax.broadcasted_iota(jnp.int32, (BEADS, BEADS), 0)
+            same = same == lax.broadcasted_iota(jnp.int32, (BEADS, BEADS), 1)
+            kinds = lax.dot_general(
+                kinds, jnp.where(same, 1.0, 0.0).astype(jnp.bfloat16), (((0,), (0,)), ((), ())),
+                preferred_element_type=jnp.float32,
+            )
+            for i in range(HALF // GROUP):
+                rows = kinds[i * GROUP:(i + 1) * GROUP]
+                for b in range(BEADS):
+                    live[s * (HALF // GROUP) + i, b * GROUP:(b + 1) * GROUP, :] = jnp.broadcast_to(
+                        rows[:, b:b + 1], (GROUP, 128)
+                    )
+
+    bead_id = (lax.broadcasted_iota(jnp.int32, (slots, GROUP * ATOMS), 0) // GROUP).astype(jnp.float32)
+    member = lax.broadcasted_iota(jnp.int32, (GROUP, GROUP * ATOMS), 1) // ATOMS
+    member = member == lax.broadcasted_iota(jnp.int32, (GROUP, GROUP * ATOMS), 0)
 
     def unit_points():
         def body(i, carry):
@@ -139,37 +196,57 @@
     def unit_beads(t):
         for i in range(per_sub):
             j = t * per_sub + i
-            onehot = jnp.where(key_ref[j:j + 1, :] == row_id, 1.0, 0.0)
+            near_atoms = repeated[j * GROUP:(j + 1) * GROUP, :]
+            own = jnp.where(member, jnp.concatenate([near_atoms, near_atoms], axis=1), -1.0)
+            onehot = jnp.where(jnp.concatenate([own] * BEADS, axis=0) == bead_id, 1.0, 0.0)
             size = jnp.maximum(jnp.sum(onehot, axis=1, keepdims=True), 1.0)
             summed = jnp.dot(onehot.astype(jnp.bfloat16), atoms[j], preferred_element_type=jnp.float32)
             inverse = 1.0 / size
             mean = jnp.sum(summed * summed, axis=1, keepdims=True) * (inverse * inverse * (1.0 / width))
             scale = inverse * lax.rsqrt(mean + EPSILON)
-            units[i * slots:(i + 1) * slots, :] = (summed * scale).astype(jnp.bfloat16)
+            units[compute_order.index(t) % 2, i * slots:(i + 1) * slots, :] = (summed * scale).astype(jnp.bfloat16)
 
     def kernel_rows(t):
         route, sub = t // 2, t % 2
         tile = 256
-
-        def body(ct, carry):
-            cols = pl.ds(pl.multiple_of(ct * tile, tile), tile)
+        for cols in (slice(i, i + tile) for i in range(0, shard, tile)):
             scores = lax.dot_general(
-                units[...], points[cols, :], (((1,), (1,)), ((), ())),
-                preferred_element_type=jnp.float32,
+                units[compute_order.index(t) % 2], points[cols, :], (((1,), (1,)), ((), ())), preferred_element_type=jnp.float32,
             )
-            kind = ptype_ref[:, cols]
+            kind = ptype[:, cols].astype(jnp.float32)
             parts = []
             for i in range(per_sub):
                 j = t * per_sub + i
                 part = jnp.exp2(scores[i * slots:(i + 1) * slots] * (LOG2E * width ** (-0.5)))
-                part = jnp.where(live_ref[:, j:j + 1] == kind, part, 0.0)
-                parts.append(jnp.sum(part.reshape(beads, GROUP, tile), axis=0))
+                alive = live[j]
+                part = jnp.where(jnp.concatenate([alive] * (tile // 128), axis=1) == kind, part, 0.0)
+                parts.append(jnp.sum(part.reshape(BEADS, GROUP, tile), axis=0))
             kbuf[route, 0, sub * SUB:(sub + 1) * SUB, cols] = jnp.concatenate(parts, axis=0).astype(jnp.bfloat16)
-            return carry
-        lax.fori_loop(0, shard // tile, body, 0)
 
     groups = [(route, outer) for outer in (0, 3, 1, 2) for route in (0, 1)]
     index_of = {group: g for g, group in enumerate(groups)}
+
+    def relative(route, step_x, step_z):
+        return (step_z % SIDE, step_x % SIDE) if route == 0 else (step_x % SIDE, step_z % SIDE)
+
+    def direct(route, n, to_x, to_z, s):
+        outer, inner = relative(route, -to_x, -to_z)
+        lanes = pl.ds(pl.multiple_of(s * STRIP, STRIP), STRIP)
+        return remote(
+            kbuf.at[route, 0, pl.ds(0, HALF), lanes],
+            rbuf.at[route, outer, pl.ds(inner * HALF, HALF), :],
+            d_send.at[route * 15 + n],
+            d_recv.at[(route * SIDE + outer) * SIDE + inner],
+            on_plane(to_x, to_z),
+        )
+
+    def direct_each(route, do):
+        for n, (to_x, to_z) in enumerate(offsets):
+            there_x, there_z = (x + to_x) % SIDE, (z + to_z) % SIDE
+
+            @pl.when(there_x // 2 == col)
+            def _():
+                do(direct(route, n, to_x, to_z, (there_x % 2) * SIDE + there_z))
 
     def strip(g, r):
         return sbuf.at[g, pl.ds(pl.multiple_of(r * STRIP, STRIP), STRIP), :]
@@ -183,33 +260,43 @@
 
     def strip_send(group):
         g = index_of[group]
+        route, outer = group
 
         @pl.when(owner)
         def _():
-            route, outer = group
-            lanes = pl.ds(pl.multiple_of(at_strip * STRIP, STRIP), STRIP)
-            mine = kbuf[route, outer, :, lanes]
-            sbuf[g, pl.ds(pl.multiple_of(row * STRIP, STRIP), STRIP), :] = mine.T
+            for inner in range(SIDE):
+                if (outer, inner) == (0, 0):
+                    lanes = pl.ds(pl.multiple_of(at_strip * STRIP, STRIP), STRIP)
+                    rbuf[route, 0, 0:HALF, :] = kbuf[route, 0, 0:HALF, lanes]
+                else:
+                    here = rbuf.at[route, outer, pl.ds(inner * HALF, HALF), :]
+                    remote(
+                        here, here, d_send.at[0], d_recv.at[(route * SIDE + outer) * SIDE + inner], sibling
+                    ).wait_recv()
+            sbuf[g, pl.ds(pl.multiple_of(row * STRIP, STRIP), STRIP), :] = rbuf[route, outer].T
             strip_copy(g, row, 0, up).start()
             strip_copy(g, row, 1, down).start()
             strip_copy(g, row, 2, sibling).start()
 
     def strip_relay(group):
         g = index_of[group]
-        other = (1 - h) * 2 + core
         r_up, r_down = h_up * 2 + core, h_down * 2 + core
 
         @pl.when(jnp.logical_not(owner))
         def _():
             strip_arrived(g, r_down)
-            strip_copy(g, r_down, 0, sibling).start()
             strip_arrived(g, r_up)
-            strip_copy(g, r_up, 1, sibling).start()
-
-            @pl.when(h == g % 2)
+
+            @pl.when(h == (g // 2) % 2)
             def _():
                 strip_copy(g, r_down, 2, up).start()
                 strip_copy(g, r_up, 3, down).start()
+            strip_copy(g, r_down, 0, sibling).start()
+            strip_copy(g, r_up, 1, sibling).start()
+
+    def strip_last(group):
+        g = index_of[group]
+        other = (1 - h) * 2 + core
 
         @pl.when(owner)
         def _():
@@ -221,7 +308,7 @@
         for which in range(2):
             strip_copy(g, row, which, sibling).wait_send()
 
-        @pl.when(jnp.logical_or(owner, h == g % 2))
+        @pl.when(jnp.logical_or(owner, h == (g // 2) % 2))
         def _():
             for which in range(2, 4):
                 strip_copy(g, row, which, sibling).wait_send()
@@ -269,77 +356,92 @@
             both = jnp.concatenate([high, wide - high], axis=0)
             sbuf[g, 4 * STRIP:, :] = both.astype(jnp.bfloat16)
 
+    prepare()
     load_points.wait()
     unit_points()
     loads[0].wait()
     unit_beads(0)
-    kernel_rows(0)
+
+    def compute(n):
+        if n + 1 < 4:
+            loads[n + 1].wait()
+            unit_beads(compute_order[n + 1])
+        kernel_rows(compute_order[n])
+
+    def gather_rest(route, outer):
+        for inner in (0, 3, 1, 2):
+            for sub in {0: (), 3: (1,), 1: (0,), 2: (0, 1)}[outer]:
+                arrived(route, outer, inner, sub)
+
+    for n in range(3):
+        compute(n)
     pl.semaphore_wait(barrier, len(peers))
-    send_own(0, 0)
+    direct_each(0, lambda copy: copy.start())
     for step in (1, 2, 3):
         weight_copy(0, step).start()
-    loads[1].wait()
-    unit_beads(2)
-    kernel_rows(2)
     send_own(1, 0)
-    loads[2].wait()
-    unit_beads(1)
-    kernel_rows(1)
+    send_own(0, 0)
+    compute(3)
+    direct_each(1, lambda copy: copy.start())
+    send_own(1, 1)
+    strip_send((0, 1))
+    strip_send((0, 0))
     send_own(0, 1)
-    inner_step(0, 3, 0)
-    inner_step(0, 1, 0)
+    near(1, 0)
+    strip_send((0, 3))
+    near(0, 0)
+    strip_send((0, 2))
+    strip_send((1, 0))
+    near(0, 1)
+    strip_send((1, 2))
+    strip_send((1, 3))
+    strip_relay((0, 3))
+    strip_relay((0, 0))
+    strip_send((1, 1))
+    strip_relay((0, 1))
+    near(1, 1)
     for step in (1, 2, 3):
         weight_copy(0, step).wait_recv()
     for step in (1, 2, 3):
         weight_copy(1, step).start()
-    loads[3].wait()
-    unit_beads(3)
-    kernel_rows(3)
-    send_own(1, 1)
-    inner_step(1, 3, 0)
-    inner_step(1, 1, 0)
-    for route in (0, 1):
-        inner_step(route, 1, 1)
-        inner_step(route, 3, 1)
-    for route in (0, 1):
-        outer_step(route, 0)
-    for route in (0, 1):
-        inner_step(route, 2, 0)
-        inner_step(route, 2, 1)
-    strip_send((0, 0))
-    strip_send((1, 0))
-    for route in (0, 1):
-        outer_step(route, 3)
+    strip_relay((0, 2))
+    middle(1, 0)
+    strip_relay((1, 0))
+    middle(0, 0)
+    middle(0, 1)
+    strip_last((0, 2))
+    strip_relay((1, 2))
+    strip_last((0, 0))
+    strip_relay((1, 3))
+    strip_relay((1, 1))
+    strip_last((1, 0))
+    middle(1, 1)
     for step in (1, 2, 3):
         weight_copy(1, step).wait_recv()
     weight_rows()
-    strip_relay((0, 0))
-    strip_relay((1, 0))
+    gather_rest(0, 0)
+    gram((0, 0), first=True)
+    strip_last((0, 1))
+    gather_rest(1, 0)
+    gram((1, 0))
+    strip_last((0, 3))
+    far(0, 0)
+    far(0, 1)
+    strip_last((1, 3))
+    strip_last((1, 1))
+    far(1, 0)
+    strip_last((1, 2))
+    gather_rest(0, 1)
+    gram((0, 1))
+    far(1, 1)
+    gather_rest(1, 1)
+    gram((1, 1))
+    gather_rest(1, 3)
+    gram((1, 3))
+    gather_rest(0, 3)
+    gram((0, 3))
     for route in (0, 1):
-        outer_step(route, 1)
-    gram((0, 0), first=True)
-    gram((1, 0))
-    for route in (0, 1):
-        outer_step(route, 2)
-    for outer, sub in ((3, 1), (1, 0)):
-        for route in (0, 1):
-            for inner in range(SIDE):
-                arrived(route, outer, inner, sub)
-            strip_send((route, outer))
-    for outer in (3, 1):
-        for route in (0, 1):
-            strip_relay((route, outer))
-    for outer in (3, 1):
-        for route in (0, 1):
-            gram((route, outer))
-    for route in (0, 1):
-        for inner in (0, 3, 1, 2):
-            for sub in (0, 1):
-                arrived(route, 2, inner, sub)
-        strip_send((route, 2))
-    for route in (0, 1):
-        strip_relay((route, 2))
-    for route in (0, 1):
+        gather_rest(route, 2)
         strips_here((route, 2))
 
     def finish(rows, cols):
@@ -353,12 +455,9 @@
         rows = pl.ds(pl.multiple_of(r * STRIP, STRIP), STRIP)
         obuf[r] = finish(rows, pl.ds(0, shard)).astype(jnp.bfloat16)
 
-    def out_copy(r, which, peer):
-        return remote(obuf.at[r], gram_out.at[row], o_send.at[which], o_recv.at[r], peer)
-
-    far = (1 - h) * 2
+    across = (1 - h) * 2
     targets = [
-        (far + core, on_y(2, core)), (far + 1 - core, on_y(2, 1 - core)), (h * 2 + 1 - core, sibling),
+        (across + core, on_y(2, core)), (across + 1 - core, on_y(2, 1 - core)), (h * 2 + 1 - core, sibling),
     ]
     for which, (r, peer) in enumerate(targets):
         block(r)
@@ -367,9 +466,11 @@
     keep = pltpu.make_async_copy(obuf.at[row], gram_out.at[row], o_local)
     keep.start()
     tail = finish(pl.ds(4 * STRIP, 16), pl.ds(0, shard))
-    rhs_out[...] = tail[0:3] + tail[8:11]
+    rhs_out[...] = tail[0:8] + tail[8:16]
     for copy in pending:
         copy.wait_send()
+    for route in (0, 1):
+        direct_each(route, lambda copy: copy.wait_send())
     for group in groups:
         strip_drain(group)
     for axis in (0, 1):
@@ -382,44 +483,52 @@
         copy.wait_recv()
 
 
+def widen(gram_in, rhs_in, gram_out, rhs_out):
+    for q in range(4):
+        gram_out[:, q, :] = gram_in[q].astype(jnp.float32)
+    rhs_out[...] = rhs_in[0:3, :]
+
+
 def shards(atom_feats, atom_bead, bead_count, bead_type, sparse_points, sparse_type, targets):
     slabs, local, atoms, width = atom_feats.shape
-    beads = bead_type.shape[-1]
     config_rows = slabs * local
     shard = sparse_points.shape[0]
     total = config_rows * lax.axis_size("dp")
     blocks = config_rows // GROUP
-    place = jnp.arange(GROUP * atoms, dtype=jnp.int32)[None, :] // atoms
-    key = atom_bead.reshape(blocks, GROUP * atoms) * GROUP + place
-    slots = jnp.arange(beads, dtype=jnp.int32)
-    live = jnp.where(slots[None, None, :] < bead_count[:, :, None], bead_type, -1)
-    live = jnp.transpose(live.reshape(blocks, GROUP, beads), (2, 1, 0)).reshape(beads * GROUP, blocks)
-    weights = jnp.transpose(targets, (1, 0, 2)).reshape(3, config_rows)
-    weights = jnp.pad(weights, ((0, 5), (0, 0)))
-    bf16, f32 = jnp.bfloat16, jnp.float32
+    bf16, f32, i32 = jnp.bfloat16, jnp.float32, jnp.int32
     dma = pltpu.SemaphoreType.DMA
     vmem = pl.BlockSpec(memory_space=pltpu.VMEM)
-    hbm = pl.BlockSpec(memory_space=pl.ANY)
+    hbm = pl.BlockSpec(memory_space=pltpu.HBM)
     gram, rhs = pl.pallas_call(
         functools.partial(kernel, total),
         out_shape=(
             jax.ShapeDtypeStruct((4, STRIP, shard), bf16),
-            jax.ShapeDtypeStruct((3, shard), f32),
+            jax.ShapeDtypeStruct((8, shard), f32),
         ),
-        in_specs=[hbm, hbm, vmem, vmem, vmem, vmem],
+        in_specs=[hbm] * 7,
         out_specs=(hbm, vmem),
         scratch_shapes=[
             pltpu.VMEM((blocks, GROUP * atoms, width), bf16),
             pltpu.VMEM((shard, width), bf16),
-            pltpu.VMEM((SUB * beads, width), bf16),
+            pltpu.VMEM((2, SUB * BEADS, width), bf16),
             pltpu.VMEM((2, SIDE, SIDE * HALF, shard), bf16),
+            pltpu.VMEM((2, SIDE, SIDE * HALF, STRIP), bf16),
             pltpu.VMEM((8, 4 * STRIP + 16, SIDE * HALF), bf16),
             pltpu.VMEM((SIDE, SIDE, 8, 128), f32),
             pltpu.VMEM((4 * STRIP + 16, shard), f32),
             pltpu.VMEM((4, STRIP, shard), bf16),
-            dma((5,)),
+            pltpu.VMEM((slabs, atoms, local), i32),
+            pltpu.VMEM(bead_count.shape, i32),
+            pltpu.VMEM((slabs, BEADS, local), i32),
+            pltpu.VMEM((1, shard), i32),
+            pltpu.VMEM((3, slabs, local), f32),
+            pltpu.VMEM((config_rows, 128), f32),
+            pltpu.VMEM((blocks, BEADS * GROUP, 128), f32),
+            dma((10,)),
             dma((60,)),
             dma((64,)),
+            dma((30,)),
+            dma((32,)),
             dma((32,)),
             dma((32,)),
             dma((6,)),
@@ -429,13 +538,30 @@
             dma,
         ],
         compiler_params=pltpu.CompilerParams(
-            collective_id=0, has_side_effects=True, vmem_limit_bytes=44 * 1024 * 1024
+            collective_id=0, has_side_effects=True, vmem_limit_bytes=60 * 1024 * 1024
         ),
     )(
-        atom_feats.reshape(blocks, GROUP * atoms, width), sparse_points, key, live,
-        sparse_type.reshape(1, shard), weights,
+        atom_feats.reshape(blocks, GROUP * atoms, width), sparse_points, jnp.swapaxes(atom_bead, 1, 2),
+        bead_count, jnp.swapaxes(bead_type, 1, 2), sparse_type.reshape(1, shard), jnp.swapaxes(targets, 0, 1),
     )
-    return (jnp.transpose(gram, (1, 0, 2)).astype(jnp.float32), rhs)
+    steps = 2
+    return pl.pallas_call(
+        widen,
+        grid=(steps,),
+        out_shape=(
+            jax.ShapeDtypeStruct((STRIP, 4, shard), f32),
+            jax.ShapeDtypeStruct((3, shard), f32),
+        ),
+        in_specs=[
+            pl.BlockSpec((4, STRIP // steps, shard), lambda i: (0, i, 0)),
+            pl.BlockSpec((8, shard), lambda i: (0, 0)),
+        ],
+        out_specs=(
+            pl.BlockSpec((STRIP // steps, 4, shard), lambda i: (i, 0, 0)),
+            pl.BlockSpec((3, shard), lambda i: (0, 0)),
+        ),
+        compiler_params=pltpu.CompilerParams(vmem_limit_bytes=60 * 1024 * 1024),
+    )(gram, rhs)
 
 
 def solution(mesh):

time: 87 us -> 64 us (0.74)
  Pallas kernels: 76.9 us -> 63.2 us
  local copies, waits for them, and re-layouts: 7.39 us -> 0 us
  other arithmetic: 1.76 us -> 0 us
    pallas_call x1, Pallas kernels: 76.9 us -> 60.6 us  [shards(): pl.pallas_call(functools.partial(kernel, total), out_shape=(jax.ShapeDtyp...]
    unnamed x7 -> x0, local copies, waits for them, and re-layouts: 6.35 us -> none
    pallas_call x0 -> x1, Pallas kernels: none -> 2.6 us  [shards(): pl.pallas_call(widen, grid=(steps,), out_shape=(jax.ShapeDtypeStruct((STR...]
where the time goes in v3:
time: 64 us; the launch traced here: 63.8 us
  Pallas kernels  63.2 us (99%)
  between operations  0.64 us (1%)
    pallas_call x1, Pallas kernels, shards(): pl.pallas_call(functools.partial(kernel, total), out_shape=(jax.ShapeDtyp...  60.6 us
    pallas_call x1, Pallas kernels, shards(): pl.pallas_call(widen, grid=(steps,), out_shape=(jax.ShapeDtypeStruct((STR...  2.6 us

profile of v3, /device:TPU:1, one launch (start us, length us, event | category | flops | bytes accessed | tf_op | source)
XLA Modules:
  0.0 63.8 jit_solution(18130989022129341828)
XLA Ops:
  0.6 60.6 %shard_map.86 = (bf16[4,128,1024]{2,1,0:T(8,128)(2,1)}, f32[8,1024]{1,0:T(8,128)}) custom-call(bf16[16,256,1024]{2,1,0:T(8,128)(2,1)} %bitcast.5, bf16[1024,1024]{1,0:T(8,128)(2,1)} %points_hbm.1, s32[2,32,64]{2,1,0:T(8,128)} %bitcast.6, s32[2,64]{1,0:T(2,128)} %count_hbm.1, s32[2,16,64]{2,1,0:T(8,128)} %bitcast.7, s32[1,1024]{1,0:T(1,128)} %bitcast.8, ...), custom_call_target="tpu_custom_call" | custom-call | tf_op jit(solution)/shard_map/pallas_call | solution.py:502
  61.2 2.6 %shard_map.87 = (f32[128,4,1024]{2,1,0:T(4,128)}, f32[3,1024]{1,0:T(4,128)}) custom-call(bf16[4,128,1024]{2,1,0:T(8,128)(2,1)} %get-tuple-element.4.gram_in, f32[8,1024]{1,0:T(8,128)} %get-tuple-element.5.rhs_in), custom_call_target="tpu_custom_call" | custom-call | tf_op jit(solution)/shard_map/pallas_call | solution.py:548

commit v4 on v3

--- a/solution.py
+++ b/solution.py
@@ -18,15 +18,18 @@
 STRIP = 128
 ATOMS = 32
 BEADS = 16
+RELAYED = ((0, 32), (32, 16))
+DIRECT = 48
+TURNS = (-1, 1)
 
 
 def kernel(
     total,
     atoms_hbm, points_hbm, bead_hbm, count_hbm, type_hbm, ptype_hbm, targets_hbm,
     gram_out, rhs_out,
-    atoms, points, units, kbuf, rbuf, sbuf, wbuf, acc, obuf,
+    atoms, points, units, kbuf, rbuf, sbuf, wbuf, acc, obuf, tbuf, relay,
     bead_in, count_in, type_in, ptype, targets_in, repeated, live,
-    load_sem, k_send, k_recv, d_send, d_recv, s_send, s_recv, w_send, w_recv, o_send, o_recv, o_local,
+    load_sem, k_send, k_recv, d_send, d_recv, s_send, s_recv, w_send, w_recv, o_send, o_recv, o_local, t_send, t_recv, y_send, y_recv, f_send, f_recv,
 ):
     width = points.shape[1]
     shard = points.shape[0]
@@ -59,7 +62,7 @@
     offsets = [(i, j) for i in range(SIDE) for j in range(SIDE) if (i, j) != (0, 0)]
 
     loads = []
-    compute_order = order = (0, 2, 1, 3)
+    compute_order = order = (0, 1, 2, 3)
     per_sub = SUB // GROUP
     small = []
     for i, (src, dst) in enumerate((
@@ -373,73 +376,74 @@
             for sub in {0: (), 3: (1,), 1: (0,), 2: (0, 1)}[outer]:
                 arrived(route, outer, inner, sub)
 
-    for n in range(3):
-        compute(n)
+    compute(0)
     pl.semaphore_wait(barrier, len(peers))
+    send_own(0, 0)
+    compute(1)
     direct_each(0, lambda copy: copy.start())
     for step in (1, 2, 3):
         weight_copy(0, step).start()
+    send_own(0, 1)
+    compute(2)
     send_own(1, 0)
-    send_own(0, 0)
     compute(3)
     direct_each(1, lambda copy: copy.start())
     send_own(1, 1)
+    strip_send((0, 0))
+    near(1, 0)
+    near(0, 0)
     strip_send((0, 1))
-    strip_send((0, 0))
-    send_own(0, 1)
-    near(1, 0)
-    strip_send((0, 3))
-    near(0, 0)
-    strip_send((0, 2))
     strip_send((1, 0))
+    strip_relay((0, 0))
     near(0, 1)
-    strip_send((1, 2))
-    strip_send((1, 3))
-    strip_relay((0, 3))
-    strip_relay((0, 0))
     strip_send((1, 1))
     strip_relay((0, 1))
+    strip_send((0, 2))
+    strip_send((1, 3))
     near(1, 1)
     for step in (1, 2, 3):
         weight_copy(0, step).wait_recv()
     for step in (1, 2, 3):
         weight_copy(1, step).start()
-    strip_relay((0, 2))
+    strip_relay((1, 0))
+    strip_send((0, 3))
+    strip_last((0, 0))
     middle(1, 0)
-    strip_relay((1, 0))
     middle(0, 0)
     middle(0, 1)
-    strip_last((0, 2))
-    strip_relay((1, 2))
-    strip_last((0, 0))
+    strip_last((1, 0))
+    strip_relay((1, 1))
+    strip_last((0, 1))
+    strip_relay((0, 2))
+    strip_send((1, 2))
+    middle(1, 1)
+    strip_relay((0, 3))
+    far(0, 0)
     strip_relay((1, 3))
-    strip_relay((1, 1))
-    strip_last((1, 0))
-    middle(1, 1)
     for step in (1, 2, 3):
         weight_copy(1, step).wait_recv()
     weight_rows()
+    gather_rest(1, 0)
+    gram((1, 0), first=True)
     gather_rest(0, 0)
-    gram((0, 0), first=True)
-    strip_last((0, 1))
-    gather_rest(1, 0)
-    gram((1, 0))
-    strip_last((0, 3))
-    far(0, 0)
+    gram((0, 0))
+    strip_relay((1, 2))
+    strip_last((1, 1))
     far(0, 1)
-    strip_last((1, 3))
-    strip_last((1, 1))
-    far(1, 0)
-    strip_last((1, 2))
     gather_rest(0, 1)
     gram((0, 1))
+    strip_last((0, 3))
+    far(1, 0)
     far(1, 1)
+    strip_last((1, 3))
+    strip_last((0, 2))
     gather_rest(1, 1)
     gram((1, 1))
+    gather_rest(0, 3)
+    gram((0, 3))
+    strip_last((1, 2))
     gather_rest(1, 3)
     gram((1, 3))
-    gather_rest(0, 3)
-    gram((0, 3))
     for route in (0, 1):
         gather_rest(route, 2)
         strips_here((route, 2))
@@ -456,12 +460,96 @@
         obuf[r] = finish(rows, pl.ds(0, shard)).astype(jnp.bfloat16)
 
     across = (1 - h) * 2
-    targets = [
-        (across + core, on_y(2, core)), (across + 1 - core, on_y(2, 1 - core)), (h * 2 + 1 - core, sibling),
-    ]
-    for which, (r, peer) in enumerate(targets):
-        block(r)
-        remote(obuf.at[r], gram_out.at[row], o_send.at[which], o_recv.at[row], peer).start()
+
+    def out_copy(r, which, peer):
+        return remote(obuf.at[r], gram_out.at[row], o_send.at[which], o_recv.at[row], peer)
+
+    def out_done(r, which):
+        copy = remote(obuf.at[r], gram_out.at[r], o_send.at[which], o_recv.at[r], sibling)
+        copy.wait_send()
+        copy.wait_recv()
+
+    def turned(s, k, do_remote, do_local):
+        there = gram_out.at[across + k, :, pl.ds(pl.multiple_of(at_strip * STRIP, STRIP), STRIP)]
+
+        @pl.when(dp != 8 * col + s)
+        def _():
+            peer = {"dp": 8 * col + s, "row": row, "col": col}
+            do_remote(remote(tbuf.at[s, k], there, t_send.at[2 * s + k], t_recv.at[2 * at_strip + k], peer))
+
+        @pl.when(dp == 8 * col + s)
+        def _():
+            do_local(pltpu.make_async_copy(tbuf.at[s, k], there, t_send.at[2 * s + k]))
+
+    def turned_arrived(s, k):
+        @pl.when(dp != 8 * col + s)
+        def _():
+            there = gram_out.at[across + k, :, pl.ds(s * STRIP, STRIP)]
+            remote(tbuf.at[s, k], there, t_send.at[2 * s + k], t_recv.at[2 * s + k], sibling).wait_recv()
+
+    def start(copy):
+        copy.start()
+
+    def turn(at_col):
+        return TURNS[0] + (TURNS[1] - TURNS[0]) * at_col
+
+    def straight(k):
+        rows = pl.ds(DIRECT, STRIP - DIRECT)
+        return remote(
+            obuf.at[across + k, rows], gram_out.at[row, rows], o_send.at[k], o_recv.at[row], on_y(2, k)
+        )
+
+    def straight_done(k):
+        rows = pl.ds(DIRECT, STRIP - DIRECT)
+        copy = remote(
+            obuf.at[across + k, rows], gram_out.at[across + k, rows], o_send.at[k], o_recv.at[across + k], sibling
+        )
+        copy.wait_send()
+        copy.wait_recv()
+
+    def first_leg(k, i):
+        rows = pl.ds(*RELAYED[i])
+        return remote(
+            obuf.at[across + k, rows], relay.at[k, rows], y_send.at[2 * k + i], y_recv.at[2 * k + i],
+            on_y(turn(col), core),
+        )
+
+    def second_leg(k, i):
+        rows = pl.ds(*RELAYED[i])
+        way = turn(1 - col)
+        source = ((y - way + SIDE) % SIDE) // 2 * 2 + core
+        return remote(
+            relay.at[k, rows], gram_out.at[source, rows], f_send.at[2 * k + i], f_recv.at[2 * core + i],
+            on_y(way, k),
+        )
+
+    def relayed_arrived(k, i):
+        here = gram_out.at[across + k, pl.ds(*RELAYED[i])]
+        remote(here, here, y_send.at[0], f_recv.at[2 * k + i], sibling).wait_recv()
+
+    for k in range(2):
+        block(across + k)
+
+        @pl.when(jnp.logical_not(owner))
+        def _():
+            for i in range(2):
+                first_leg(k, i).start()
+            straight(k).start()
+
+        @pl.when(owner)
+        def _():
+            for s in range(8):
+                tbuf[s, k] = obuf[across + k, :, s * STRIP:(s + 1) * STRIP].T
+                turned(s, k, start, start)
+    block(h * 2 + 1 - core)
+    out_copy(h * 2 + 1 - core, 2, sibling).start()
+
+    @pl.when(owner)
+    def _():
+        for k in range(2):
+            for i in range(2):
+                first_leg(k, i).wait_recv()
+                second_leg(k, i).start()
     block(row)
     keep = pltpu.make_async_copy(obuf.at[row], gram_out.at[row], o_local)
     keep.start()
@@ -477,10 +565,25 @@
         for step in (1, 2, 3):
             weight_copy(axis, step).wait_send()
     keep.wait()
-    for which, (r, peer) in enumerate(targets):
-        copy = remote(obuf.at[r], gram_out.at[r], o_send.at[which], o_recv.at[r], peer)
-        copy.wait_send()
-        copy.wait_recv()
+    out_done(h * 2 + 1 - core, 2)
+
+    @pl.when(jnp.logical_not(owner))
+    def _():
+        for k in range(2):
+            straight_done(k)
+            for i in range(2):
+                first_leg(k, i).wait_send()
+                relayed_arrived(k, i)
+
+    @pl.when(owner)
+    def _():
+        for k in range(2):
+            for i in range(2):
+                second_leg(k, i).wait_send()
+        for s in range(8):
+            for k in range(2):
+                turned(s, k, lambda copy: copy.wait_send(), lambda copy: copy.wait())
+                turned_arrived(s, k)
 
 
 def widen(gram_in, rhs_in, gram_out, rhs_out):
@@ -517,6 +620,8 @@
             pltpu.VMEM((SIDE, SIDE, 8, 128), f32),
             pltpu.VMEM((4 * STRIP + 16, shard), f32),
             pltpu.VMEM((4, STRIP, shard), bf16),
+            pltpu.VMEM((8, 2, STRIP, STRIP), bf16),
+            pltpu.VMEM((2, DIRECT, shard), bf16),
             pltpu.VMEM((slabs, atoms, local), i32),
             pltpu.VMEM(bead_count.shape, i32),
             pltpu.VMEM((slabs, BEADS, local), i32),
@@ -536,6 +641,12 @@
             dma((3,)),
             dma((4,)),
             dma,
+            dma((16,)),
+            dma((16,)),
+            dma((4,)),
+            dma((4,)),
+            dma((4,)),
+            dma((4,)),
         ],
         compiler_params=pltpu.CompilerParams(
             collective_id=0, has_side_effects=True, vmem_limit_bytes=60 * 1024 * 1024

time: 64 us -> 57.4 us (0.90)
  the two profiles are of different devices: /device:TPU:1 before, /device:TPU:9 now
where the time goes in v4:
time: 57.4 us; the launch traced here: 57.2 us
  Pallas kernels  56.6 us (99%)
  between operations  0.64 us (1%)
    pallas_call x1, Pallas kernels, shards(): pl.pallas_call(functools.partial(kernel, total), out_shape=(jax.ShapeDtyp...  54 us
    pallas_call x1, Pallas kernels, shards(): pl.pallas_call(widen, grid=(steps,), out_shape=(jax.ShapeDtypeStruct((STR...  2.6 us

profile of v4, /device:TPU:9, one launch (start us, length us, event | category | flops | bytes accessed | tf_op | source)
XLA Modules:
  0.0 57.2 jit_solution(8457335884451356223)
XLA Ops:
  0.6 54.0 %shard_map.86 = (bf16[4,128,1024]{2,1,0:T(8,128)(2,1)}, f32[8,1024]{1,0:T(8,128)}) custom-call(bf16[16,256,1024]{2,1,0:T(8,128)(2,1)} %bitcast.5, bf16[1024,1024]{1,0:T(8,128)(2,1)} %points_hbm.1, s32[2,32,64]{2,1,0:T(8,128)} %bitcast.6, s32[2,64]{1,0:T(2,128)} %count_hbm.1, s32[2,16,64]{2,1,0:T(8,128)} %bitcast.7, s32[1,1024]{1,0:T(1,128)} %bitcast.8, ...), custom_call_target="tpu_custom_call" | custom-call | tf_op jit(solution)/shard_map/pallas_call | solution.py:605
  54.6 2.6 %shard_map.87 = (f32[128,4,1024]{2,1,0:T(4,128)}, f32[3,1024]{1,0:T(4,128)}) custom-call(bf16[4,128,1024]{2,1,0:T(8,128)(2,1)} %get-tuple-element.4.gram_in, f32[8,1024]{1,0:T(8,128)} %get-tuple-element.5.rhs_in), custom_call_target="tpu_custom_call" | custom-call | tf_op jit(solution)/shard_map/pallas_call | solution.py:659

commit v5 on v4

--- a/solution.py
+++ b/solution.py
@@ -387,63 +387,63 @@
     compute(2)
     send_own(1, 0)
     compute(3)
+    send_own(1, 1)
     direct_each(1, lambda copy: copy.start())
-    send_own(1, 1)
+    strip_send((0, 1))
+    strip_send((0, 2))
     strip_send((0, 0))
+    strip_send((0, 3))
     near(1, 0)
     near(0, 0)
-    strip_send((0, 1))
     strip_send((1, 0))
+    strip_relay((0, 1))
+    near(0, 1)
     strip_relay((0, 0))
-    near(0, 1)
-    strip_send((1, 1))
-    strip_relay((0, 1))
-    strip_send((0, 2))
-    strip_send((1, 3))
+    strip_relay((0, 2))
     near(1, 1)
     for step in (1, 2, 3):
         weight_copy(0, step).wait_recv()
     for step in (1, 2, 3):
         weight_copy(1, step).start()
+    strip_relay((0, 3))
     strip_relay((1, 0))
-    strip_send((0, 3))
-    strip_last((0, 0))
+    strip_send((1, 3))
+    strip_send((1, 2))
+    strip_send((1, 1))
     middle(1, 0)
     middle(0, 0)
+    strip_relay((1, 3))
+    strip_last((0, 0))
     middle(0, 1)
-    strip_last((1, 0))
+    strip_relay((1, 2))
+    middle(1, 1)
     strip_relay((1, 1))
     strip_last((0, 1))
-    strip_relay((0, 2))
-    strip_send((1, 2))
-    middle(1, 1)
-    strip_relay((0, 3))
-    far(0, 0)
-    strip_relay((1, 3))
+    strip_last((1, 0))
     for step in (1, 2, 3):
         weight_copy(1, step).wait_recv()
     weight_rows()
+    gather_rest(0, 0)
+    gram((0, 0), first=True)
     gather_rest(1, 0)
-    gram((1, 0), first=True)
-    gather_rest(0, 0)
-    gram((0, 0))
-    strip_relay((1, 2))
-    strip_last((1, 1))
+    gram((1, 0))
+    far(1, 0)
+    strip_last((0, 3))
     far(0, 1)
+    strip_last((1, 3))
+    strip_last((0, 2))
+    far(0, 0)
     gather_rest(0, 1)
     gram((0, 1))
-    strip_last((0, 3))
-    far(1, 0)
     far(1, 1)
-    strip_last((1, 3))
-    strip_last((0, 2))
+    strip_last((1, 1))
+    gather_rest(1, 3)
+    gram((1, 3))
+    strip_last((1, 2))
+    gather_rest(0, 3)
+    gram((0, 3))
     gather_rest(1, 1)
     gram((1, 1))
-    gather_rest(0, 3)
-    gram((0, 3))
-    strip_last((1, 2))
-    gather_rest(1, 3)
-    gram((1, 3))
     for route in (0, 1):
         gather_rest(route, 2)
         strips_here((route, 2))

time: 57.4 us -> 55.4 us (0.965)
  the two profiles are of different devices: /device:TPU:9 before, /device:TPU:1 now
where the time goes in v5:
time: 55.4 us; the launch traced here: 55.2 us
  Pallas kernels  54.6 us (99%)
  between operations  0.64 us (1%)
    pallas_call x1, Pallas kernels, shards(): pl.pallas_call(functools.partial(kernel, total), out_shape=(jax.ShapeDtyp...  52 us
    pallas_call x1, Pallas kernels, shards(): pl.pallas_call(widen, grid=(steps,), out_shape=(jax.ShapeDtypeStruct((STR...  2.6 us

profile of v5, /device:TPU:1, one launch (start us, length us, event | category | flops | bytes accessed | tf_op | source)
XLA Modules:
  0.0 55.2 jit_solution(16369514798561861163)
XLA Ops:
  0.6 52.0 %shard_map.86 = (bf16[4,128,1024]{2,1,0:T(8,128)(2,1)}, f32[8,1024]{1,0:T(8,128)}) custom-call(bf16[16,256,1024]{2,1,0:T(8,128)(2,1)} %bitcast.5, bf16[1024,1024]{1,0:T(8,128)(2,1)} %points_hbm.1, s32[2,32,64]{2,1,0:T(8,128)} %bitcast.6, s32[2,64]{1,0:T(2,128)} %count_hbm.1, s32[2,16,64]{2,1,0:T(8,128)} %bitcast.7, s32[1,1024]{1,0:T(1,128)} %bitcast.8, ...), custom_call_target="tpu_custom_call" | custom-call | tf_op jit(solution)/shard_map/pallas_call | solution.py:605
  52.6 2.6 %shard_map.87 = (f32[128,4,1024]{2,1,0:T(4,128)}, f32[3,1024]{1,0:T(4,128)}) custom-call(bf16[4,128,1024]{2,1,0:T(8,128)(2,1)} %get-tuple-element.4.gram_in, f32[8,1024]{1,0:T(8,128)} %get-tuple-element.5.rhs_in), custom_call_target="tpu_custom_call" | custom-call | tf_op jit(solution)/shard_map/pallas_call | solution.py:659

commit v6 on v5

--- a/solution.py
+++ b/solution.py
@@ -77,7 +77,8 @@
     for t in order:
         rows = pl.ds(t * per_sub, per_sub)
         copy = pltpu.make_async_copy(atoms_hbm.at[rows], atoms.at[rows], load_sem.at[t])
-        copy.start()
+        if len(loads) < 1:
+            copy.start()
         loads.append(copy)
 
     barrier = pltpu.get_barrier_semaphore()
@@ -361,12 +362,17 @@
 
     prepare()
     load_points.wait()
+    for copy in loads[1:]:
+        copy.start()
     unit_points()
     loads[0].wait()
     unit_beads(0)
 
     def compute(n):
-        if n + 1 < 4:
+        if n == 1:
+            loads[1].wait()
+            unit_beads(compute_order[1])
+        if 0 < n < 3:
             loads[n + 1].wait()
             unit_beads(compute_order[n + 1])
         kernel_rows(compute_order[n])

time: 55.4 us -> 55.3 us (level)
  no operation moved by 1% of the time
where the time goes in v6:
time: 55.3 us; the launch traced here: 55.1 us
  Pallas kernels  54.5 us (99%)
  between operations  0.64 us (1%)
    pallas_call x1, Pallas kernels, shards(): pl.pallas_call(functools.partial(kernel, total), out_shape=(jax.ShapeDtyp...  51.9 us
    pallas_call x1, Pallas kernels, shards(): pl.pallas_call(widen, grid=(steps,), out_shape=(jax.ShapeDtypeStruct((STR...  2.6 us

profile of v6, /device:TPU:1, one launch (start us, length us, event | category | flops | bytes accessed | tf_op | source)
XLA Modules:
  0.0 55.1 jit_solution(7550381998225123395)
XLA Ops:
  0.6 51.9 %shard_map.86 = (bf16[4,128,1024]{2,1,0:T(8,128)(2,1)}, f32[8,1024]{1,0:T(8,128)}) custom-call(bf16[16,256,1024]{2,1,0:T(8,128)(2,1)} %bitcast.5, bf16[1024,1024]{1,0:T(8,128)(2,1)} %points_hbm.1, s32[2,32,64]{2,1,0:T(8,128)} %bitcast.6, s32[2,64]{1,0:T(2,128)} %count_hbm.1, s32[2,16,64]{2,1,0:T(8,128)} %bitcast.7, s32[1,1024]{1,0:T(1,128)} %bitcast.8, ...), custom_call_target="tpu_custom_call" | custom-call | tf_op jit(solution)/shard_map/pallas_call | solution.py:611
  52.5 2.6 %shard_map.87 = (f32[128,4,1024]{2,1,0:T(4,128)}, f32[3,1024]{1,0:T(4,128)}) custom-call(bf16[4,128,1024]{2,1,0:T(8,128)(2,1)} %get-tuple-element.4.gram_in, f32[8,1024]{1,0:T(8,128)} %get-tuple-element.5.rhs_in), custom_call_target="tpu_custom_call" | custom-call | tf_op jit(solution)/shard_map/pallas_call | solution.py:665
